TPU v7x, 32 devices: a whole 2x2x4 slice. The times are simulated.
32 devices in a mesh: dp: 8 (over z, y), expert: 4 (over x, core).
Axes of the slice: x: 2, y: 2, z: 4, core: 2. Of those that a mesh axis runs over, the one named last changes fastest.
Arguments:
- tokens: bfloat16 [4096, 2048], P(('dp', 'expert')), may hold values from -6 to 6
- expert_ids: int32 [4096, 2], P(('dp', 'expert')), may hold values from 0 to 3, all different within a row; in each aligned block of 128 rows (0 to 127, 128 to 255, ...) at most 96 rows name the same one
- gates: float32 [4096, 2], P(('dp', 'expert')), may hold values from 0.2 to 1
- w_in: bfloat16 [4, 2048, 1536], P('expert'), may hold values from -0.125 to 0.125
- w_out: bfloat16 [4, 768, 2048], P('expert'), may hold values from -0.21875 to 0.21875
- out_grad: bfloat16 [4096, 2048], P(('dp', 'expert')), may hold values from -6 to 6
Outputs:
- mixed: bfloat16 [4096, 2048], P(('dp', 'expert'))
- token_grad: bfloat16 [4096, 2048], P(('dp', 'expert'))
- gate_grad: float32 [4096, 2], P(('dp', 'expert'))
- w_in_grad: bfloat16 [4, 2048, 1536], P('expert', 'dp')
- w_out_grad: bfloat16 [4, 768, 2048], P('expert', 'dp')
Inputs may be any that keep to these rules, and one draw needn't show every extreme that they name: `expert_ids`: the 2 ids of a token differ. Among the 128 tokens of one device no expert is named more than 96 times, and in every draw some expert is named exactly 96 times by the tokens of some device.
All inputs are finite; a program needn't handle non-finite values.
Results may differ from a plain program's by a relative error of at most 0.0065.
Values may be sent and summed in bfloat16 or wider, within the bound.
A program may use at most 128 MiB of HBM per device.

v0:
```python
import jax
import jax.numpy as jnp
from jax import lax
from jax.sharding import PartitionSpec as P


def swiglu_forward(gate_up, hidden_width):
    gate_part = gate_up[:, :hidden_width]
    up_part = gate_up[:, hidden_width:]
    return (gate_part, up_part, (jax.nn.silu(gate_part) * up_part).astype(jnp.bfloat16))


def swiglu_backward(grad_hidden, gate_part, up_part):
    sigmoid_gate = jax.nn.sigmoid(gate_part)
    silu_gate = gate_part * sigmoid_gate
    grad_gate = grad_hidden * up_part * (sigmoid_gate * (1.0 + gate_part * (1.0 - sigmoid_gate)))
    grad_up = grad_hidden * silu_gate
    return jnp.concatenate([grad_gate, grad_up], axis=1).astype(jnp.bfloat16)


def per_device(tokens, expert_ids, gates, w_in, w_out, out_grad):
    groups = lax.axis_size("expert")
    my_group = lax.axis_index("expert")
    token_rows, model_width = tokens.shape
    top_count = expert_ids.shape[1]
    hidden_width = w_out.shape[1]
    capacity = 3 * token_rows * top_count // (2 * groups)
    entries = token_rows * top_count
    flat_ids = expert_ids.reshape(entries)
    one_hot = (flat_ids[:, None] == jnp.arange(groups, dtype=jnp.int32)[None, :]).astype(jnp.int32)
    slot_rank = jnp.sum((jnp.cumsum(one_hot, axis=0) - one_hot) * one_hot, axis=1)
    dest_slot = flat_ids * capacity + slot_rank
    source_entry = (
        jnp.full((groups * capacity,), entries, jnp.int32)
        .at[dest_slot]
        .set(jnp.arange(entries, dtype=jnp.int32))
    )
    filled = source_entry < entries
    clamped_entry = jnp.minimum(source_entry, entries - 1)
    weight_in = w_in[0]
    weight_out = w_out[0]
    zero_value = jnp.zeros((), jnp.bfloat16)
    group_tok, group_ids = (
        lax.all_gather(tokens, "expert", axis=0, tiled=True),
        lax.all_gather(expert_ids.astype(jnp.bfloat16), "expert", axis=0, tiled=True),
    )
    ids_by_source = group_ids.astype(jnp.int32).reshape(groups, entries)
    is_mine = (ids_by_source == my_group).astype(jnp.int32)
    my_ranks = jnp.cumsum(is_mine, axis=1) - is_mine
    my_slots = jnp.where(is_mine > 0, my_ranks, capacity)
    source_index = jnp.broadcast_to(jnp.arange(groups, dtype=jnp.int32)[:, None], (groups, entries))
    entry_index = jnp.broadcast_to(jnp.arange(entries, dtype=jnp.int32)[None, :], (groups, entries))
    picked_entry = (
        jnp.full((groups, capacity), entries, jnp.int32)
        .at[source_index, my_slots]
        .set(entry_index, mode="drop")
    )
    picked_valid = picked_entry < entries
    picked_rows = (
        jnp.arange(groups, dtype=jnp.int32)[:, None] * token_rows
        + jnp.minimum(picked_entry, entries - 1) // top_count
    )
    received = jnp.where(picked_valid[..., None], group_tok[picked_rows], zero_value)
    received = received.reshape(groups * capacity, model_width)
    gate_up = jnp.dot(received, weight_in, preferred_element_type=jnp.float32)
    gate_part, up_part, hidden = swiglu_forward(gate_up, hidden_width)
    expert_out = jnp.dot(hidden, weight_out, preferred_element_type=jnp.float32).astype(
        jnp.bfloat16
    )
    returned = lax.all_to_all(
        expert_out.reshape(groups, capacity, model_width),
        "expert",
        split_axis=0,
        concat_axis=0,
        tiled=True,
    )
    returned = returned.reshape(groups * capacity, model_width)
    per_entry = returned[dest_slot].reshape(token_rows, top_count, model_width).astype(jnp.float32)
    upstream = out_grad.astype(jnp.float32)
    mixed = jnp.sum(gates[:, :, None] * per_entry, axis=1).astype(jnp.bfloat16)
    gate_grad = jnp.sum(per_entry * upstream[:, None, :], axis=2)
    grad_entries = (
        (gates[:, :, None] * upstream[:, None, :])
        .astype(jnp.bfloat16)
        .reshape(entries, model_width)
    )
    send_grads = jnp.where(filled[:, None], grad_entries[clamped_entry], zero_value)
    grad_rows = lax.all_to_all(
        send_grads.reshape(groups, capacity, model_width),
        "expert",
        split_axis=0,
        concat_axis=0,
        tiled=True,
    )
    grad_rows = grad_rows.reshape(groups * capacity, model_width)
    grad_hidden = jnp.dot(grad_rows, weight_out.T, preferred_element_type=jnp.float32)
    grad_gate_up = swiglu_backward(grad_hidden, gate_part, up_part)
    grad_inputs = jnp.dot(grad_gate_up, weight_in.T, preferred_element_type=jnp.float32).astype(
        jnp.bfloat16
    )
    grad_back = lax.all_to_all(
        grad_inputs.reshape(groups, capacity, model_width),
        "expert",
        split_axis=0,
        concat_axis=0,
        tiled=True,
    )
    grad_back = grad_back.reshape(groups * capacity, model_width)
    token_grad = jnp.sum(
        grad_back[dest_slot].reshape(token_rows, top_count, model_width).astype(jnp.float32), axis=1
    ).astype(jnp.bfloat16)
    grad_w_out = jnp.dot(hidden.T, grad_rows, preferred_element_type=jnp.float32)
    grad_w_in = jnp.dot(received.T, grad_gate_up, preferred_element_type=jnp.float32)
    shard_in, shard_out = (
        lax.psum_scatter(grad_w_in[None], "dp", scatter_dimension=1, tiled=True),
        lax.psum_scatter(grad_w_out[None], "dp", scatter_dimension=1, tiled=True),
    )
    return (
        mixed,
        token_grad,
        gate_grad,
        shard_in.astype(jnp.bfloat16),
        shard_out.astype(jnp.bfloat16),
    )


def solution(mesh):
    placed = (
        P(("dp", "expert"), None),
        P(("dp", "expert"), None),
        P(("dp", "expert"), None),
        P("expert", None, None),
        P("expert", None, None),
        P(("dp", "expert"), None),
    )
    return jax.shard_map(
        per_device,
        mesh=mesh,
        in_specs=placed,
        out_specs=(
            P(("dp", "expert"), None),
            P(("dp", "expert"), None),
            P(("dp", "expert"), None),
            P("expert", "dp", None),
            P("expert", "dp", None),
        ),
        check_vma=False,
    )
```

profile of v0, /device:TPU:0, one launch (start us, length us, event | category | flops | bytes accessed | tf_op | source)
XLA Modules:
  0.0 431.8 jit_solution(11544478817778071205)
XLA Ops:
  7.2 0.7 all-gather.2.cloned.1.call-update
  7.9 0.9 broadcast_multiply_fusion
  8.8 0.8 copy.33
  9.6 0.1 eq.47
  9.7 0.1 eq.43
  9.9 0.1 copy.32
  10.0 0.1 mul.92
  10.2 1.2 reduce-window.16
  11.8 1.4 scatter_custom_fusion
  13.2 0.8 copy.27
  14.0 0.1 mul.95
  14.3 3.4 mul.97
  17.7 3.7 mul.98
  21.4 2.7 multiply_convert_fusion
  24.1 6.4 %gather_fusion.2 = bf16[384,2048]{1,0:T(8,128)(2,1)} fusion(bf16[256,2048]{1,0:T(8,128)(2,1)} %multiply_convert_fusion, s32[1024]{0:T(1024)S(1)} %pad_clamp_fusion), kind=kCustom, calls=%fused_computation.2 | custom fusion | bytes 3147264 | tf_op jit(solution)/shard_map/gather | solution.py:87
  30.6 2.7 broadcast_select_fusion
  33.3 4.5 %all-to-all-start.1 = ((bf16[4,96,2048]{2,1,0:T(8,128)(2,1)}), bf16[4,96,2048]{2,1,0:T(8,128)(2,1)}, u32[]{:S(2)}, u32[]{:S(2)}) async-start(bf16[4,96,2048]{2,1,0:T(8,128)(2,1)} %broadcast_select_fusion), calls=%async_computation.1 | async-start | bytes 3145728 | tf_op jit(solution)/shard_map/all_to_all | solution.py:88
  37.9 21.6 %all_gather.6 = bf16[512,2]{0,1:T(2,128)(2,1)S(1)} all-gather(bf16[128,2]{0,1:T(2,128)(2,1)S(1)} %get-tuple-element.16), channel_id=1, replica_groups=mesh['dp'=8,'expert'=4] {'expert'}, dimensions={0}, use_global_device_ids=true | all-gather | bytes 2560 | tf_op jit(solution)/shard_map/all_gather | solution.py:45
  59.4 0.1 copy.28
  59.6 0.2 reshape.232
  59.8 0.2 reshape.231
  60.0 1.2 reduce-window.14
  61.8 4.5 %scatter_custom_fusion.1 = s32[384]{0:T(512)S(1)} fusion(s32[1024]{0:T(1024)S(1)} %bitcast.73, s32[1024]{0:T(1024)S(1)} %bitcast.72, s32[]{:T(128)} %constant.17.clone.1), kind=kCustom, calls=%fused_computation.66 | custom fusion | bytes 1540
  66.7 6.9 %gather_fusion = bf16[384,2048]{1,0:T(8,128)(2,1)} fusion(bf16[512,2048]{1,0:T(8,128)(2,1)} %all-gather.2.cloned.1.call-done, s32[1024]{0:T(1024)S(1)} %pad_clamp_fusion.2), kind=kCustom, calls=%fused_computation | custom fusion | bytes 3147264 | tf_op jit(solution)/shard_map/gather | solution.py:63
  73.6 1.6 broadcast_select_fusion.1
  75.2 6.8 %fusion.2 = f32[384,1536]{1,0:T(8,128)} fusion(bf16[384,2048]{1,0:T(8,128)(2,1)S(1)} %bitcast.67, bf16[1,2048,1536]{2,1,0:T(8,128)(2,1)} %param.9), kind=kOutput, calls=%fused_computation.9 | convolution fusion | flops 2415919104 | bytes 10223616 | tf_op jit(solution)/shard_map/dot_general | solution.py:65
  82.0 4.8 %multiply_convert_fusion.2 = (bf16[384,768]{1,0:T(8,128)(2,1)}, bf16[384,768]{1,0:T(8,128)(2,1)}, bf16[384,768]{1,0:T(8,128)(2,1)S(1)}) fusion(f32[384,1536]{1,0:T(8,128)} %fusion.2, bf16[384,2048]{1,0:T(8,128)(2,1)} %bitcast.12, bf16[1,768,2048]{2,1,0:T(8,128)(2,1)S(1)} %copy-done), kind=kOutput, calls=%fused_computation.27 | convolution fusion | flops 1212383232 | bytes 8847360 | tf_op jit(solution)/shard_map/dot_general | solution.py:96
  86.8 0.9 copy-done.1
  87.7 5.8 %convolution_bitcast_fusion.1 = f32[1,768,2048]{2,1,0:T(8,128)} fusion(bf16[384,768]{1,0:T(8,128)(2,1)S(1)} %get-tuple-element.14, bf16[384,2048]{1,0:T(8,128)(2,1)} %bitcast.12), kind=kOutput, calls=%fused_computation.11 | convolution fusion | flops 1207959552 | bytes 8454144 | tf_op jit(solution)/shard_map/dot_general | solution.py:112
  93.6 10.0 %convolution_bitcast_fusion = f32[1,2048,1536]{2,1,0:T(8,128)} fusion(bf16[384,2048]{1,0:T(8,128)(2,1)} %gather_fusion, pred[384]{0:T(512)(128)(4,1)S(1)} %broadcast_compare_fusion, bf16[384,768]{1,0:T(8,128)(2,1)} %get-tuple-element.13, bf16[384,768]{1,0:T(8,128)(2,1)} %get-tuple-element.12), kind=kOutput, calls=%fused_computation.6 | convolution fusion | flops 2419064832 | bytes 15335808 | tf_op jit(solution)/shard_map/dot_general | solution.py:113
  103.6 7.0 %fusion.11 = bf16[384,2048]{1,0:T(8,128)(2,1)} fusion(bf16[1,2048,1536]{2,1,0:T(8,128)(2,1)} %param.9, bf16[384,768]{1,0:T(8,128)(2,1)} %get-tuple-element.13, bf16[384,768]{1,0:T(8,128)(2,1)} %get-tuple-element.12), kind=kOutput, calls=%fused_computation.17 | convolution fusion | flops 2419064832 | bytes 9043968 | tf_op jit(solution)/shard_map/dot_general | solution.py:98
  110.6 4.3 %all-to-all-start.2 = ((bf16[4,96,2048]{2,1,0:T(8,128)(2,1)}), bf16[4,96,2048]{2,1,0:T(8,128)(2,1)}, u32[]{:S(2)}, u32[]{:S(2)}) async-start(bf16[4,96,2048]{2,1,0:T(8,128)(2,1)} %bitcast.66), calls=%async_computation.2 | async-start | bytes 3145728 | tf_op jit(solution)/shard_map/all_to_all | solution.py:101
  115.0 3.6 fusion.8
  118.6 16.5 %all-to-all-done.2 = bf16[4,96,2048]{2,1,0:T(8,128)(2,1)} async-done(((bf16[4,96,2048]{2,1,0:T(8,128)(2,1)}), bf16[4,96,2048]{2,1,0:T(8,128)(2,1)}, u32[]{:S(2)}, u32[]{:S(2)}) %all-to-all-start.2) | async-done | bytes 1572896 | tf_op jit(solution)/shard_map/all_to_all | solution.py:101
  135.1 4.3 %all-to-all-start = ((bf16[4,96,2048]{2,1,0:T(8,128)(2,1)}), bf16[4,96,2048]{2,1,0:T(8,128)(2,1)}, u32[]{:S(2)}, u32[]{:S(2)}) async-start(bf16[4,96,2048]{2,1,0:T(8,128)(2,1)} %bitcast.65), calls=%async_computation | async-start | bytes 3145728 | tf_op jit(solution)/shard_map/all_to_all | solution.py:70
  139.5 2.2 convert_element_type.83
  141.7 5.0 %gather_fusion.3 = bf16[256,2048]{1,0:T(8,128)(2,1)} fusion(bf16[384,2048]{1,0:T(8,128)(2,1)} %bitcast.14, s32[1024]{0:T(1024)S(1)} %pad_clamp_fusion.1), kind=kCustom, calls=%fused_computation.3 | custom fusion | bytes 2098176 | tf_op jit(solution)/shard_map/gather | solution.py:110
  146.7 2.5 reshape.226
  149.2 10.4 %all-to-all-done = bf16[4,96,2048]{2,1,0:T(8,128)(2,1)} async-done(((bf16[4,96,2048]{2,1,0:T(8,128)(2,1)}), bf16[4,96,2048]{2,1,0:T(8,128)(2,1)}, u32[]{:S(2)}, u32[]{:S(2)}) %all-to-all-start) | async-done | bytes 1572896 | tf_op jit(solution)/shard_map/all_to_all | solution.py:70
  159.6 5.0 %gather_fusion.1 = bf16[256,2048]{1,0:T(8,128)(2,1)} fusion(bf16[384,2048]{1,0:T(8,128)(2,1)} %bitcast.6, s32[1024]{0:T(1024)S(1)} %pad_clamp_fusion.1), kind=kCustom, calls=%fused_computation.1 | custom fusion | bytes 2098176 | tf_op jit(solution)/shard_map/gather | solution.py:78
  164.6 3.4 reshape.237
  168.0 6.3 %multiply_reduce_fusion = (f32[128,2]{1,0:T(8,128)S(1)}, bf16[128,2048]{1,0:T(8,128)(2,1)}) fusion(f32[128,2,2048]{2,1,0:T(2,128)} %reshape.237, f32[128,2048]{1,0:T(8,128)} %convert_element_type.83, f32[128,2]{1,0:T(8,128)S(1)} %copy.27), kind=kLoop, calls=%fused_computation.18 | loop fusion | flops 1834752 | bytes 3672064 | tf_op jit(solution)/shard_map/reduce_sum | solution.py:81
  174.2 0.6 copy.38
  174.9 4.6 %reduce_sum.44 = bf16[128,2048]{1,0:T(8,128)(2,1)} reduce(bf16[128,2,2048]{2,1,0:T(2,128)(2,1)} %reshape.226, bf16[]{:T(256)} %constant.30.clone.1), dimensions={1}, to_apply=%region_8.9 | reduce | flops 262144 | bytes 1572866 | tf_op jit(solution)/shard_map/reduce_sum | solution.py:109
  179.5 33.3 %reduce-scatter.5.cloned.1.call-done = f32[1,96,2048]{2,1,0:T(8,128)} async-done(((f32[1,768,2048]{2,1,0:T(8,128)}), f32[1,96,2048]{2,1,0:T(8,128)}) %reduce-scatter.5.cloned.1.call-update) | async-done | bytes 786448 | tf_op jit(solution)/shard_map/reduce_scatter | solution.py:116
  212.7 1.9 convert_element_type.87
  214.7 208.2 %reduce-scatter.3.cloned.1.call-done = f32[1,256,1536]{2,1,0:T(8,128)} async-done(((f32[1,2048,1536]{2,1,0:T(8,128)}), f32[1,256,1536]{2,1,0:T(8,128)}) %reduce-scatter.3.cloned.1.call-update) | async-done | bytes 1572880 | tf_op jit(solution)/shard_map/reduce_scatter | solution.py:115
  422.9 2.4 convert_element_type.86
  (53 shorter events, 1.7 us)
Async XLA Ops:
  7.2 74.8 %copy-start = (bf16[1,768,2048]{2,1,0:T(8,128)(2,1)S(1)}, bf16[1,768,2048]{2,1,0:T(8,128)(2,1)}, u32[]{:S(2)}) copy-start(bf16[1,768,2048]{2,1,0:T(8,128)(2,1)} %param.10) | copy-start | bytes 9437188
  7.2 59.5 %all-gather.2.cloned.1.call-start = ((), (), s32[]{:S(2)}) async-start(), calls=%async_computation.5 | async-start | bytes 2621440 | tf_op jit(solution)/shard_map/all_gather | solution.py:44
  33.3 28.3 %copy-start.3 = (s32[2]{0:T(128)S(1)}, s32[2]{0:T(128)}, u32[]{:S(2)}) copy-start(s32[2]{0:T(128)} %constant.59) | copy-start | bytes 28
  33.3 28.4 %copy-start.2 = (s32[2]{0:T(128)S(1)}, s32[2]{0:T(128)}, u32[]{:S(2)}) copy-start(s32[2]{0:T(128)} %constant.62) | copy-start | bytes 28
  33.3 48.6 %all-to-all-start.1 = ((bf16[4,96,2048]{2,1,0:T(8,128)(2,1)}), bf16[4,96,2048]{2,1,0:T(8,128)(2,1)}, u32[]{:S(2)}, u32[]{:S(2)}) async-start(bf16[4,96,2048]{2,1,0:T(8,128)(2,1)} %broadcast_select_fusion), calls=%async_computation.1 | async-start | bytes 3145728 | tf_op jit(solution)/shard_map/all_to_all | solution.py:88
  37.8 174.9 %reduce-scatter.5.cloned.1.call-start = ((), (), s32[]{:S(2)}) async-start(), calls=%async_computation.7 | async-start | bytes 7077888 | tf_op jit(solution)/shard_map/reduce_scatter | solution.py:116
  86.8 0.9 copy-start.1
  93.6 329.3 %reduce-scatter.3.cloned.1.call-start = ((), (), s32[]{:S(2)}) async-start(), calls=%async_computation.6 | async-start | bytes 14155776 | tf_op jit(solution)/shard_map/reduce_scatter | solution.py:115
  110.6 24.5 %all-to-all-start.2 = ((bf16[4,96,2048]{2,1,0:T(8,128)(2,1)}), bf16[4,96,2048]{2,1,0:T(8,128)(2,1)}, u32[]{:S(2)}, u32[]{:S(2)}) async-start(bf16[4,96,2048]{2,1,0:T(8,128)(2,1)} %bitcast.66), calls=%async_computation.2 | async-start | bytes 3145728 | tf_op jit(solution)/shard_map/all_to_all | solution.py:101
  135.1 24.5 %all-to-all-start = ((bf16[4,96,2048]{2,1,0:T(8,128)(2,1)}), bf16[4,96,2048]{2,1,0:T(8,128)(2,1)}, u32[]{:S(2)}, u32[]{:S(2)}) async-start(bf16[4,96,2048]{2,1,0:T(8,128)(2,1)} %bitcast.65), calls=%async_computation | async-start | bytes 3145728 | tf_op jit(solution)/shard_map/all_to_all | solution.py:70
Sparse Core Ops, SparseCore 0:
  9.6 25.2 all-gather.1
  93.7 119.0 reduce-scatter.4
  216.3 206.5 reduce-scatter.2
where the time goes:
time: 433 us; the launch traced here: 432 us
  waiting for transfers between devices  269 us (62%)
  local copies, waits for them, and re-layouts  47.5 us (11%)
  matrix products  38.1 us (9%)
  other arithmetic  28.3 us (7%)
  blocking collectives  21.6 us (5%)
  between operations  13.9 us (3%)
  starting transfers between devices  13.3 us (3%)
    reduce_scatter x1, waiting for transfers between devices, per_device(): lax.psum_scatter(grad_w_in[None], 'dp', scatter_dimension=1, tiled=True)  208 us
    reduce_scatter x1, waiting for transfers between devices, per_device(): lax.psum_scatter(grad_w_out[None], 'dp', scatter_dimension=1, tiled=True)  33.3 us
    all_gather x1, blocking collectives, per_device(): lax.all_gather(expert_ids.astype(jnp.bfloat16), 'expert', axis=0, tiled=T...  21.6 us
    all_to_all x1, waiting for transfers between devices, per_device(): lax.all_to_all(grad_inputs.reshape(groups, capacity, model_width), 'exper...  16.5 us
    all_to_all x1, waiting for transfers between devices, per_device(): lax.all_to_all(expert_out.reshape(groups, capacity, model_width), 'expert...  10.4 us
    dot_general x1, matrix products, per_device(): jnp.dot(received.T, grad_gate_up, preferred_element_type=jnp.float32)  10 us
  transfers between devices with their start and end apart: 6, of which 4 were waited for; matrix products, arithmetic and copies ran while one was open for 23% of the time, Pallas kernels for 0%

commit v1 on v0

--- a/solution.py
+++ b/solution.py
@@ -112,8 +112,8 @@
     grad_w_out = jnp.dot(hidden.T, grad_rows, preferred_element_type=jnp.float32)
     grad_w_in = jnp.dot(received.T, grad_gate_up, preferred_element_type=jnp.float32)
     shard_in, shard_out = (
-        lax.psum_scatter(grad_w_in[None], "dp", scatter_dimension=1, tiled=True),
-        lax.psum_scatter(grad_w_out[None], "dp", scatter_dimension=1, tiled=True),
+        lax.psum_scatter(grad_w_in.astype(jnp.bfloat16)[None], "dp", scatter_dimension=1, tiled=True),
+        lax.psum_scatter(grad_w_out.astype(jnp.bfloat16)[None], "dp", scatter_dimension=1, tiled=True),
     )
     return (
         mixed,

time: 433 us -> 297 us (0.69)
  waiting for transfers between devices: 269 us -> 140 us
    reduce_scatter x2, waiting for transfers between devices: 241 us -> 113 us  [the longest x1 113 us: per_device(): lax.psum_scatter(grad_w_in.astype(jnp.bfloat16)[None], 'dp', scatter_dime...]
  transfers between devices with their start and end apart: 6 -> 6, of which waited for: 4 -> 3; matrix products, arithmetic and copies ran while one was open for 23% -> 32% of each run, Pallas kernels for 0% -> 0%
where the time goes in v1:
time: 297 us; the launch traced here: 296 us
  waiting for transfers between devices  140 us (47%)
  local copies, waits for them, and re-layouts  47.4 us (16%)
  matrix products  35.2 us (12%)
  other arithmetic  24 us (8%)
  blocking collectives  21.6 us (7%)
  between operations  13.9 us (5%)
  starting transfers between devices  13.8 us (5%)
    reduce_scatter x1, waiting for transfers between devices, per_device(): lax.psum_scatter(grad_w_in.astype(jnp.bfloat16)[None], 'dp', scatter_dime...  113 us
    all_gather x1, blocking collectives, per_device(): lax.all_gather(expert_ids.astype(jnp.bfloat16), 'expert', axis=0, tiled=T...  21.6 us
    all_to_all x1, waiting for transfers between devices, per_device(): lax.all_to_all(grad_inputs.reshape(groups, capacity, model_width), 'exper...  16.5 us
    all_to_all x1, waiting for transfers between devices, per_device(): lax.all_to_all(expert_out.reshape(groups, capacity, model_width), 'expert...  10.2 us
    dot_general x1, matrix products, per_device(): jnp.dot(received.T, grad_gate_up, preferred_element_type=jnp.float32)  7.96 us
    unnamed x15, local copies, waits for them, and re-layouts  7.52 us
    mul x2, local copies, waits for them, and re-layouts, per_device(): gates[:, :, None] * upstream[:, None, :]  7.14 us
    dot_general x1, matrix products, per_device(): jnp.dot(grad_gate_up, weight_in.T, preferred_element_type=jnp.float32)  6.96 us
  transfers between devices with their start and end apart: 6, of which 3 were waited for; matrix products, arithmetic and copies ran while one was open for 32% of the time, Pallas kernels for 0%

profile of v1, /device:TPU:0, one launch (start us, length us, event | category | flops | bytes accessed | tf_op | source)
XLA Modules:
  0.0 296.4 jit_solution(18318994725317898974)
XLA Ops:
  7.2 0.7 all-gather.2.cloned.1.call-update
  7.9 0.9 broadcast_multiply_fusion
  8.8 0.8 copy.33
  9.6 0.1 eq.47
  9.7 0.1 eq.43
  9.9 0.1 copy.32
  10.0 0.1 mul.92
  10.2 1.2 reduce-window.16
  11.5 0.1 copy.35
  11.8 1.4 scatter_custom_fusion
  13.2 0.8 copy.27
  14.0 0.1 mul.95
  14.3 3.4 %mul.97 = f32[128,2,2048]{2,1,0:T(2,128)} broadcast(bf16[128,2048]{1,0:T(8,128)(2,1)} %param.11), dimensions={0,2} | broadcast | bytes 2621440 | tf_op jit(solution)/shard_map/mul | solution.py:83
  17.7 3.7 %mul.98 = f32[256,2048]{1,0:T(8,128)} reshape(f32[128,2,2048]{2,1,0:T(2,128)} %mul.97) | data formatting | bytes 4194304 | tf_op jit(solution)/shard_map/mul | solution.py:83
  21.4 2.7 multiply_convert_fusion
  24.1 6.4 %gather_fusion.2 = bf16[384,2048]{1,0:T(8,128)(2,1)} fusion(bf16[256,2048]{1,0:T(8,128)(2,1)} %multiply_convert_fusion, s32[1024]{0:T(1024)S(1)} %pad_clamp_fusion), kind=kCustom, calls=%fused_computation.2 | custom fusion | bytes 3147264 | tf_op jit(solution)/shard_map/gather | solution.py:87
  30.6 2.7 broadcast_select_fusion
  33.3 4.5 %all-to-all-start.1 = ((bf16[4,96,2048]{2,1,0:T(8,128)(2,1)}), bf16[4,96,2048]{2,1,0:T(8,128)(2,1)}, u32[]{:S(2)}, u32[]{:S(2)}) async-start(bf16[4,96,2048]{2,1,0:T(8,128)(2,1)} %broadcast_select_fusion), calls=%async_computation.1 | async-start | bytes 3145728 | tf_op jit(solution)/shard_map/all_to_all | solution.py:88
  37.9 21.6 %all_gather.6 = bf16[512,2]{0,1:T(2,128)(2,1)S(1)} all-gather(bf16[128,2]{0,1:T(2,128)(2,1)S(1)} %get-tuple-element.16), channel_id=1, replica_groups=mesh['dp'=8,'expert'=4] {'expert'}, dimensions={0}, use_global_device_ids=true | all-gather | bytes 2560 | tf_op jit(solution)/shard_map/all_gather | solution.py:45
  59.4 0.1 copy.28
  59.6 0.2 reshape.232
  59.8 0.2 reshape.231
  59.9 1.2 reduce-window.14
  61.3 0.1 copy.30
  61.8 4.5 %scatter_custom_fusion.1 = s32[384]{0:T(512)S(1)} fusion(s32[1024]{0:T(1024)S(1)} %bitcast.73, s32[1024]{0:T(1024)S(1)} %bitcast.72, s32[]{:T(128)} %constant.17.clone.1), kind=kCustom, calls=%fused_computation.68 | custom fusion | bytes 1540
  66.7 6.9 %gather_fusion = bf16[384,2048]{1,0:T(8,128)(2,1)} fusion(bf16[512,2048]{1,0:T(8,128)(2,1)} %all-gather.2.cloned.1.call-done, s32[1024]{0:T(1024)S(1)} %pad_clamp_fusion.2), kind=kCustom, calls=%fused_computation | custom fusion | bytes 3147264 | tf_op jit(solution)/shard_map/gather | solution.py:63
  73.6 1.6 broadcast_select_fusion.1
  75.2 6.8 %fusion.3 = f32[384,1536]{1,0:T(8,128)} fusion(bf16[384,2048]{1,0:T(8,128)(2,1)S(1)} %bitcast.67, bf16[1,2048,1536]{2,1,0:T(8,128)(2,1)} %param.9), kind=kOutput, calls=%fused_computation.10 | convolution fusion | flops 2415919104 | bytes 10223616 | tf_op jit(solution)/shard_map/dot_general | solution.py:65
  82.0 4.9 %multiply_convert_fusion.2 = (bf16[384,768]{1,0:T(8,128)(2,1)}, bf16[384,768]{1,0:T(8,128)(2,1)}, bf16[384,768]{1,0:T(8,128)(2,1)S(1)}) fusion(f32[384,1536]{1,0:T(8,128)} %fusion.3, bf16[384,2048]{1,0:T(8,128)(2,1)} %bitcast.12, bf16[1,768,2048]{2,1,0:T(8,128)(2,1)S(1)} %copy-done), kind=kOutput, calls=%fused_computation.29 | convolution fusion | flops 1212383232 | bytes 8847360 | tf_op jit(solution)/shard_map/dot_general | solution.py:96
  86.9 0.8 copy-done.3
  87.7 4.9 %fusion.9 = bf16[1,768,2048]{2,1,0:T(8,128)(2,1)} fusion(bf16[384,768]{1,0:T(8,128)(2,1)S(1)} %get-tuple-element.14, bf16[384,2048]{1,0:T(8,128)(2,1)} %bitcast.12), kind=kOutput, calls=%fused_computation.17 | convolution fusion | flops 1209532416 | bytes 5308416 | tf_op jit(solution)/shard_map/dot_general | solution.py:112
  92.7 0.3 reduce-scatter.3.cloned.1.call-start
  92.9 8.0 %fusion = bf16[1,2048,1536]{2,1,0:T(8,128)(2,1)} fusion(bf16[384,2048]{1,0:T(8,128)(2,1)} %gather_fusion, pred[384]{0:T(512)(128)(4,1)S(1)} %broadcast_compare_fusion, bf16[384,768]{1,0:T(8,128)(2,1)} %get-tuple-element.13, bf16[384,768]{1,0:T(8,128)(2,1)} %get-tuple-element.12), kind=kOutput, calls=%fused_computation.7 | convolution fusion | flops 2422210560 | bytes 9044352 | tf_op jit(solution)/shard_map/dot_general | solution.py:113
  100.9 7.0 %fusion.13 = bf16[384,2048]{1,0:T(8,128)(2,1)} fusion(bf16[1,2048,1536]{2,1,0:T(8,128)(2,1)} %param.9, bf16[384,768]{1,0:T(8,128)(2,1)} %get-tuple-element.13, bf16[384,768]{1,0:T(8,128)(2,1)} %get-tuple-element.12), kind=kOutput, calls=%fused_computation.19 | convolution fusion | flops 2419064832 | bytes 9043968 | tf_op jit(solution)/shard_map/dot_general | solution.py:98
  107.9 4.4 %all-to-all-start.2 = ((bf16[4,96,2048]{2,1,0:T(8,128)(2,1)}), bf16[4,96,2048]{2,1,0:T(8,128)(2,1)}, u32[]{:S(2)}, u32[]{:S(2)}) async-start(bf16[4,96,2048]{2,1,0:T(8,128)(2,1)} %bitcast.66), calls=%async_computation.2 | async-start | bytes 3145728 | tf_op jit(solution)/shard_map/all_to_all | solution.py:101
  112.3 3.6 %fusion.10 = bf16[384,2048]{1,0:T(8,128)(2,1)} fusion(bf16[384,768]{1,0:T(8,128)(2,1)} %copy-done.3, bf16[1,768,2048]{2,1,0:T(8,128)(2,1)S(1)} %copy-done), kind=kOutput, calls=%fused_computation.18 | convolution fusion | flops 1208745984 | bytes 5308416 | tf_op jit(solution)/shard_map/dot_general | solution.py:67
  115.9 16.5 %all-to-all-done.2 = bf16[4,96,2048]{2,1,0:T(8,128)(2,1)} async-done(((bf16[4,96,2048]{2,1,0:T(8,128)(2,1)}), bf16[4,96,2048]{2,1,0:T(8,128)(2,1)}, u32[]{:S(2)}, u32[]{:S(2)}) %all-to-all-start.2) | async-done | bytes 1572896 | tf_op jit(solution)/shard_map/all_to_all | solution.py:101
  132.4 4.6 %all-to-all-start = ((bf16[4,96,2048]{2,1,0:T(8,128)(2,1)}), bf16[4,96,2048]{2,1,0:T(8,128)(2,1)}, u32[]{:S(2)}, u32[]{:S(2)}) async-start(bf16[4,96,2048]{2,1,0:T(8,128)(2,1)} %bitcast.65), calls=%async_computation | async-start | bytes 3145728 | tf_op jit(solution)/shard_map/all_to_all | solution.py:70
  137.0 2.1 convert_element_type.83
  139.2 5.0 %gather_fusion.3 = bf16[256,2048]{1,0:T(8,128)(2,1)} fusion(bf16[384,2048]{1,0:T(8,128)(2,1)} %bitcast.14, s32[1024]{0:T(1024)S(1)} %pad_clamp_fusion.1), kind=kCustom, calls=%fused_computation.3 | custom fusion | bytes 2098176 | tf_op jit(solution)/shard_map/gather | solution.py:110
  144.2 2.6 reshape.226
  146.8 10.2 %all-to-all-done = bf16[4,96,2048]{2,1,0:T(8,128)(2,1)} async-done(((bf16[4,96,2048]{2,1,0:T(8,128)(2,1)}), bf16[4,96,2048]{2,1,0:T(8,128)(2,1)}, u32[]{:S(2)}, u32[]{:S(2)}) %all-to-all-start) | async-done | bytes 1572896 | tf_op jit(solution)/shard_map/all_to_all | solution.py:70
  156.9 5.0 %gather_fusion.1 = bf16[256,2048]{1,0:T(8,128)(2,1)} fusion(bf16[384,2048]{1,0:T(8,128)(2,1)} %bitcast.6, s32[1024]{0:T(1024)S(1)} %pad_clamp_fusion.1), kind=kCustom, calls=%fused_computation.1 | custom fusion | bytes 2098176 | tf_op jit(solution)/shard_map/gather | solution.py:78
  161.9 3.3 %reshape.237 = f32[128,2,2048]{2,1,0:T(2,128)} reshape(bf16[256,2048]{1,0:T(8,128)(2,1)} %gather_fusion.1) | data formatting | bytes 3145728 | tf_op jit(solution)/shard_map/convert_element_type | solution.py:78
  165.3 6.3 %multiply_reduce_fusion = (f32[128,2]{1,0:T(8,128)S(1)}, bf16[128,2048]{1,0:T(8,128)(2,1)}) fusion(f32[128,2,2048]{2,1,0:T(2,128)} %reshape.237, f32[128,2048]{1,0:T(8,128)} %convert_element_type.83, f32[128,2]{1,0:T(8,128)S(1)} %copy.27), kind=kLoop, calls=%fused_computation.20 | loop fusion | flops 1834752 | bytes 3672064 | tf_op jit(solution)/shard_map/reduce_sum | solution.py:81
  171.5 0.6 copy.38
  172.2 4.6 %reduce_sum.44 = bf16[128,2048]{1,0:T(8,128)(2,1)} reduce(bf16[128,2,2048]{2,1,0:T(2,128)(2,1)} %reshape.226, bf16[]{:T(256)} %constant.30.clone.1), dimensions={1}, to_apply=%region_8.9 | reduce | flops 262144 | bytes 1572866 | tf_op jit(solution)/shard_map/reduce_sum | solution.py:109
  176.7 113.1 %reduce-scatter.3.cloned.1.call-done = bf16[1,256,1536]{2,1,0:T(8,128)(2,1)} async-done(((bf16[1,2048,1536]{2,1,0:T(8,128)(2,1)}), bf16[1,256,1536]{2,1,0:T(8,128)(2,1)}) %reduce-scatter.3.cloned.1.call-update) | async-done | bytes 786448 | tf_op jit(solution)/shard_map/reduce_scatter | solution.py:115
  (51 shorter events, 1.5 us)
Async XLA Ops:
  7.2 74.8 %copy-start = (bf16[1,768,2048]{2,1,0:T(8,128)(2,1)S(1)}, bf16[1,768,2048]{2,1,0:T(8,128)(2,1)}, u32[]{:S(2)}) copy-start(bf16[1,768,2048]{2,1,0:T(8,128)(2,1)} %param.10) | copy-start | bytes 9437188
  7.2 59.5 %all-gather.2.cloned.1.call-start = ((), (), s32[]{:S(2)}) async-start(), calls=%async_computation.5 | async-start | bytes 2621440 | tf_op jit(solution)/shard_map/all_gather | solution.py:44
  33.3 28.3 %copy-start.2 = (s32[2]{0:T(128)S(1)}, s32[2]{0:T(128)}, u32[]{:S(2)}) copy-start(s32[2]{0:T(128)} %constant.59) | copy-start | bytes 28
  33.3 28.4 %copy-start.1 = (s32[2]{0:T(128)S(1)}, s32[2]{0:T(128)}, u32[]{:S(2)}) copy-start(s32[2]{0:T(128)} %constant.62) | copy-start | bytes 28
  33.3 48.7 %all-to-all-start.1 = ((bf16[4,96,2048]{2,1,0:T(8,128)(2,1)}), bf16[4,96,2048]{2,1,0:T(8,128)(2,1)}, u32[]{:S(2)}, u32[]{:S(2)}) async-start(bf16[4,96,2048]{2,1,0:T(8,128)(2,1)} %broadcast_select_fusion), calls=%async_computation.1 | async-start | bytes 3145728 | tf_op jit(solution)/shard_map/all_to_all | solution.py:88
  37.8 138.9 %reduce-scatter.5.cloned.1.call-start = ((), (), s32[]{:S(2)}) async-start(), calls=%async_computation.7 | async-start | bytes 3538944 | tf_op jit(solution)/shard_map/reduce_scatter | solution.py:116
  86.9 0.8 copy-start.3
  92.7 197.2 %reduce-scatter.3.cloned.1.call-start = ((), (), s32[]{:S(2)}) async-start(), calls=%async_computation.6 | async-start | bytes 7077888 | tf_op jit(solution)/shard_map/reduce_scatter | solution.py:115
  107.9 24.5 %all-to-all-start.2 = ((bf16[4,96,2048]{2,1,0:T(8,128)(2,1)}), bf16[4,96,2048]{2,1,0:T(8,128)(2,1)}, u32[]{:S(2)}, u32[]{:S(2)}) async-start(bf16[4,96,2048]{2,1,0:T(8,128)(2,1)} %bitcast.66), calls=%async_computation.2 | async-start | bytes 3145728 | tf_op jit(solution)/shard_map/all_to_all | solution.py:101
  132.4 24.5 %all-to-all-start = ((bf16[4,96,2048]{2,1,0:T(8,128)(2,1)}), bf16[4,96,2048]{2,1,0:T(8,128)(2,1)}, u32[]{:S(2)}, u32[]{:S(2)}) async-start(bf16[4,96,2048]{2,1,0:T(8,128)(2,1)} %bitcast.65), calls=%async_computation | async-start | bytes 3145728 | tf_op jit(solution)/shard_map/all_to_all | solution.py:70
Sparse Core Ops, SparseCore 0:
  9.6 25.2 all-gather.1
  92.8 75.7 reduce-scatter.4
  172.7 117.0 reduce-scatter.2

commit v2 on v1

v2 whole, which is shorter than its diff:
```python
import jax
import jax.numpy as jnp
from jax import lax
from jax.sharding import PartitionSpec as P


def swiglu_forward(gate_up, hidden_width):
    gate_part = gate_up[:, :hidden_width]
    up_part = gate_up[:, hidden_width:]
    return (gate_part, up_part, (jax.nn.silu(gate_part) * up_part).astype(jnp.bfloat16))


def swiglu_backward(grad_hidden, gate_part, up_part):
    sigmoid_gate = jax.nn.sigmoid(gate_part)
    silu_gate = gate_part * sigmoid_gate
    grad_gate = grad_hidden * up_part * (sigmoid_gate * (1.0 + gate_part * (1.0 - sigmoid_gate)))
    grad_up = grad_hidden * silu_gate
    return jnp.concatenate([grad_gate, grad_up], axis=1).astype(jnp.bfloat16)


def halving_sum(parts, axis):
    count = lax.axis_size(axis)
    me = lax.axis_index(axis)
    bit = 1
    while bit < count:
        mine = (me // bit) % 2
        pairs = parts.reshape((parts.shape[0] // 2, 2) + parts.shape[1:])
        keep = lax.dynamic_index_in_dim(pairs, mine, axis=1, keepdims=False)
        send = lax.dynamic_index_in_dim(pairs, 1 - mine, axis=1, keepdims=False)
        came = lax.ppermute(
            send.astype(jnp.bfloat16), axis, [(i, i ^ bit) for i in range(count)]
        )
        parts = keep.astype(jnp.float32) + came.astype(jnp.float32)
        bit *= 2
    return parts[0].astype(jnp.bfloat16)


def per_device(tokens, expert_ids, gates, w_in, w_out, out_grad):
    groups = lax.axis_size("expert")
    shards = lax.axis_size("dp")
    token_rows, model_width = tokens.shape
    top_count = expert_ids.shape[1]
    hidden_width = w_out.shape[1]
    capacity = 3 * token_rows * top_count // (2 * groups)
    slots = groups * capacity
    weight_in = w_in[0]
    weight_out = w_out[0]
    ids = expert_ids.T
    gate_rows = gates.T
    named = ids[:, None, :] == jnp.arange(groups, dtype=jnp.int32)[None, :, None]
    member = jnp.any(named, axis=0)
    order = jnp.arange(token_rows, dtype=jnp.int32)
    earlier = (order[:, None] < order[None, :]).astype(jnp.bfloat16)
    rank = jnp.dot(
        member.astype(jnp.bfloat16), earlier, preferred_element_type=jnp.float32
    ).astype(jnp.int32)
    slot_of = jnp.where(member, rank, -1)
    taken = slot_of[:, None, :] == jnp.arange(capacity, dtype=jnp.int32)[None, :, None]
    gate_of = jnp.sum(jnp.where(named, gate_rows[:, None, :], 0.0), axis=0)
    slot_gate = jnp.sum(jnp.where(taken, gate_of[:, None, :], 0.0), axis=2).reshape(slots, 1)
    pick = taken.astype(jnp.bfloat16).reshape(slots, token_rows)

    def exchange(rows):
        return lax.all_to_all(
            rows.reshape(groups, capacity, model_width),
            "expert",
            split_axis=0,
            concat_axis=0,
            tiled=True,
        ).reshape(slots, model_width)

    received = exchange(
        jnp.dot(pick, tokens, preferred_element_type=jnp.float32).astype(jnp.bfloat16)
    )
    grad_rows = exchange(
        (jnp.dot(pick, out_grad, preferred_element_type=jnp.float32) * slot_gate).astype(
            jnp.bfloat16
        )
    )
    gate_up = jnp.dot(received, weight_in, preferred_element_type=jnp.float32)
    gate_part, up_part, hidden = swiglu_forward(gate_up, hidden_width)
    grad_hidden = jnp.dot(grad_rows, weight_out.T, preferred_element_type=jnp.float32)
    grad_gate_up = swiglu_backward(grad_hidden, gate_part, up_part)
    grad_w_in = jnp.dot(received.T, grad_gate_up, preferred_element_type=jnp.float32)
    shard_in = lax.psum_scatter(
        grad_w_in.astype(jnp.bfloat16)[None], "dp", scatter_dimension=1, tiled=True
    )
    grad_w_out = jnp.dot(hidden.T, grad_rows, preferred_element_type=jnp.float32)
    shard_out = halving_sum(
        grad_w_out.reshape(shards, hidden_width // shards, model_width), "dp"
    )[None]
    returned = exchange(
        jnp.dot(hidden, weight_out, preferred_element_type=jnp.float32).astype(jnp.bfloat16)
    )
    grad_back = exchange(
        jnp.dot(grad_gate_up, weight_in.T, preferred_element_type=jnp.float32).astype(
            jnp.bfloat16
        )
    )
    first_slot = jnp.arange(groups, dtype=jnp.int32)[:, None] * capacity
    dest_slot = jnp.sum(jnp.where(named, (first_slot + rank)[None], 0), axis=1)
    home = dest_slot[:, :, None] == jnp.arange(slots, dtype=jnp.int32)[None, None, :]
    per_entry = jnp.dot(
        home.astype(jnp.bfloat16).reshape(top_count * token_rows, slots),
        returned,
        preferred_element_type=jnp.float32,
    ).reshape(top_count, token_rows, model_width)
    upstream = out_grad.astype(jnp.float32)
    mixed = jnp.sum(gate_rows[:, :, None] * per_entry, axis=0).astype(jnp.bfloat16)
    gate_grad = jnp.sum(per_entry * upstream[None], axis=2).T
    token_grad = jnp.dot(
        jnp.any(home, axis=0).astype(jnp.bfloat16), grad_back, preferred_element_type=jnp.float32
    ).astype(jnp.bfloat16)
    return (mixed, token_grad, gate_grad, shard_in, shard_out)


def solution(mesh):
    placed = (
        P(("dp", "expert"), None),
        P(("dp", "expert"), None),
        P(("dp", "expert"), None),
        P("expert", None, None),
        P("expert", None, None),
        P(("dp", "expert"), None),
    )
    return jax.shard_map(
        per_device,
        mesh=mesh,
        in_specs=placed,
        out_specs=(
            P(("dp", "expert"), None),
            P(("dp", "expert"), None),
            P(("dp", "expert"), None),
            P("expert", "dp", None),
            P("expert", "dp", None),
        ),
        check_vma=False,
    )
```

time: 297 us -> 219 us (0.74)
  local copies, waits for them, and re-layouts: 47.4 us -> 12 us
  waiting for transfers between devices: 140 us -> 111 us
  blocking collectives: 21.6 us -> 0 us
  other arithmetic: 24 us -> 9.74 us
  starting transfers between devices: 13.8 us -> 25.5 us
  matrix products: 35.2 us -> 45.7 us
    reduce_scatter x1, waiting for transfers between devices: 113 us -> 5.62 us  [per_device(): lax.psum_scatter(grad_w_in.astype(jnp.bfloat16)[None], 'dp', scatter_dime...]
    ppermute x0 -> x3, waiting for transfers between devices: none -> 69.7 us  [halving_sum(): lax.ppermute(send.astype(jnp.bfloat16), axis, [(i, i ^ bit) for i in rang...]
    gather x4 -> x0, local copies, waits for them, and re-layouts: 23.4 us -> none  [the longest x1 6.95 us: per_device(): group_tok[picked_rows]]
    all_gather x1 -> x0, blocking collectives: 21.6 us -> none  [per_device(): lax.all_gather(expert_ids.astype(jnp.bfloat16), 'expert', axis=0, tiled=T...]
    dot_general x0 -> x5, matrix products: none -> 11.7 us  [the longest x1 3.31 us: per_device(): jnp.dot(home.astype(jnp.bfloat16).reshape(top_count * token_rows, slots),...]
    reduce_sum x3, other arithmetic: 10.9 us -> 0.17 us  [the longest x1 0.14 us: per_device(): jnp.sum(jnp.where(taken, gate_of[:, None, :], 0.0), axis=2)]
    all_to_all x3 -> x4, waiting for transfers between devices: 26.7 us -> 36 us  [exchange(): lax.all_to_all(rows.reshape(groups, capacity, model_width), 'expert', spl...]
    ppermute x0 -> x3, starting transfers between devices: none -> 7.88 us  [halving_sum(): lax.ppermute(send.astype(jnp.bfloat16), axis, [(i, i ^ bit) for i in rang...]
  transfers between devices with their start and end apart: 6 -> 8, of which waited for: 3 -> 7; matrix products, arithmetic and copies ran while one was open for 32% -> 21% of each run, Pallas kernels for 0% -> 0%
where the time goes in v2:
time: 219 us
  waiting for transfers between devices  111 us (51%)
  matrix products  45.7 us (21%)
  starting transfers between devices  25.5 us (12%)
  between operations  14.2 us (6%)
  local copies, waits for them, and re-layouts  12 us (5%)
  other arithmetic  9.74 us (4%)
    ppermute x3, waiting for transfers between devices, halving_sum(): lax.ppermute(send.astype(jnp.bfloat16), axis, [(i, i ^ bit) for i in rang...  69.7 us
    all_to_all x4, waiting for transfers between devices, exchange(): lax.all_to_all(rows.reshape(groups, capacity, model_width), 'expert', spl...  36 us
    all_to_all x4, starting transfers between devices, exchange(): lax.all_to_all(rows.reshape(groups, capacity, model_width), 'expert', spl...  17.6 us
    dot_general x1, matrix products, per_device(): jnp.dot(grad_gate_up, weight_in.T, preferred_element_type=jnp.float32)  8.21 us
    ppermute x3, starting transfers between devices, halving_sum(): lax.ppermute(send.astype(jnp.bfloat16), axis, [(i, i ^ bit) for i in rang...  7.88 us
    dot_general x1, matrix products, per_device(): gate_up = jnp.dot(received, weight_in, preferred_element_type=jnp.float32)  7.28 us
    dot_general x1, matrix products, per_device(): jnp.dot(received.T, grad_gate_up, preferred_element_type=jnp.float32)  6.89 us
    unnamed x24, local copies, waits for them, and re-layouts  6.51 us
  transfers between devices with their start and end apart: 8, of which 7 were waited for; matrix products, arithmetic and copies ran while one was open for 21% of the time, Pallas kernels for 0%

profile of v2, /device:TPU:0, one launch (start us, length us, event | category | flops | bytes accessed | tf_op | source)
XLA Modules:
  0.0 218.5 jit_solution(5182554095379428859)
XLA Ops:
  7.2 0.0 copy-start
  7.2 0.8 fusion.23
  8.0 0.1 eq.87
  8.1 0.1 broadcast_add_fusion
  8.2 0.2 bitcast_compare_fusion
  8.4 2.8 %convolution_convert_fusion.1 = bf16[384,2048]{1,0:T(8,128)(2,1)} fusion(pred[384,128]{1,0:T(32,128)(4,1)S(1)} %bitcast_compare_fusion, bf16[128,2048]{1,0:T(8,128)(2,1)} %param.6), kind=kOutput, calls=%fused_computation.15 | convolution fusion | flops 202113024 | bytes 2146304 | tf_op jit(solution)/shard_map/dot_general | solution.py:73
  11.2 4.5 %all-to-all-start = ((bf16[4,96,2048]{2,1,0:T(8,128)(2,1)}), bf16[4,96,2048]{2,1,0:T(8,128)(2,1)}, u32[]{:S(2)}, u32[]{:S(2)}) async-start(bf16[4,96,2048]{2,1,0:T(8,128)(2,1)} %bitcast.74), calls=%async_computation | async-start | bytes 3145728 | tf_op jit(solution)/shard_map/all_to_all | solution.py:64
  15.7 0.1 select_reduce_fusion
  15.8 0.1 mul.62
  15.9 2.8 %multiply_convert_fusion = bf16[384,2048]{1,0:T(8,128)(2,1)} fusion(pred[384,128]{1,0:T(32,128)(4,1)S(1)} %bitcast_compare_fusion, bf16[128,2048]{1,0:T(8,128)(2,1)} %param.11, f32[384]{0:T(512)S(1)} %mul.62), kind=kOutput, calls=%fused_computation.12 | convolution fusion | flops 202899456 | bytes 2147840 | tf_op jit(solution)/shard_map/dot_general | solution.py:76
  18.7 17.7 %all-to-all-done = bf16[4,96,2048]{2,1,0:T(8,128)(2,1)} async-done(((bf16[4,96,2048]{2,1,0:T(8,128)(2,1)}), bf16[4,96,2048]{2,1,0:T(8,128)(2,1)}, u32[]{:S(2)}, u32[]{:S(2)}) %all-to-all-start) | async-done | bytes 1572896 | tf_op jit(solution)/shard_map/all_to_all | solution.py:64
  36.4 4.4 %all-to-all-start.2 = ((bf16[4,96,2048]{2,1,0:T(8,128)(2,1)}), bf16[4,96,2048]{2,1,0:T(8,128)(2,1)}, u32[]{:S(2)}, u32[]{:S(2)}) async-start(bf16[4,96,2048]{2,1,0:T(8,128)(2,1)} %bitcast.73), calls=%async_computation.2 | async-start | bytes 3145728 | tf_op jit(solution)/shard_map/all_to_all | solution.py:64
  40.7 0.0 reduce-scatter.2.cloned.1.call-start
  40.8 7.3 %fusion.3 = f32[384,1536]{1,0:T(8,128)} fusion(bf16[384,2048]{1,0:T(8,128)(2,1)} %bitcast.5, bf16[1,2048,1536]{2,1,0:T(8,128)(2,1)} %param.9), kind=kOutput, calls=%fused_computation.4 | convolution fusion | flops 2415919104 | bytes 10223616 | tf_op jit(solution)/shard_map/dot_general | solution.py:80
  48.1 12.8 %all-to-all-done.2 = bf16[4,96,2048]{2,1,0:T(8,128)(2,1)} async-done(((bf16[4,96,2048]{2,1,0:T(8,128)(2,1)}), bf16[4,96,2048]{2,1,0:T(8,128)(2,1)}, u32[]{:S(2)}, u32[]{:S(2)}) %all-to-all-start.2) | async-done | bytes 1572896 | tf_op jit(solution)/shard_map/all_to_all | solution.py:64
  60.9 4.7 %multiply_convert_fusion.2 = (bf16[384,768]{1,0:T(8,128)(2,1)S(1)}, bf16[384,768]{1,0:T(8,128)(2,1)S(1)}, bf16[384,768]{1,0:T(8,128)(2,1)}) fusion(f32[384,1536]{1,0:T(8,128)} %fusion.3, bf16[384,2048]{1,0:T(8,128)(2,1)} %bitcast.12, bf16[1,768,2048]{2,1,0:T(8,128)(2,1)S(1)} %copy-done), kind=kOutput, calls=%fused_computation.24 | convolution fusion | flops 1212383232 | bytes 8847360 | tf_op jit(solution)/shard_map/dot_general | solution.py:82
  65.5 0.8 copy-done.8
  66.4 0.2 copy-done.10
  66.6 6.9 %fusion = bf16[1,2048,1536]{2,1,0:T(8,128)(2,1)} fusion(bf16[384,2048]{1,0:T(8,128)(2,1)} %bitcast.5, bf16[384,768]{1,0:T(8,128)(2,1)S(1)} %get-tuple-element.8, bf16[384,768]{1,0:T(8,128)(2,1)S(1)} %get-tuple-element.7), kind=kOutput, calls=%fused_computation.1 | convolution fusion | flops 2421424128 | bytes 9043968 | tf_op jit(solution)/shard_map/dot_general | solution.py:84
  73.5 0.0 reduce-scatter.2.cloned.1.call-update
  73.5 2.1 copy.15
  75.7 3.4 %fusion.26 = f32[4,2,96,2048]{3,2,1,0:T(8,128)S(1)} fusion(bf16[4,2,96,384]{3,2,1,0:T(8,128)(2,1)} %bitcast.75, bf16[384,2048,1,1]{1,0,3,2:T(8,128)(2,1)} %bitcast.20), kind=kOutput, calls=%fused_computation.51 | convolution fusion | flops 1207959552 | bytes 8454144 | tf_op jit(solution)/shard_map/dot_general | solution.py:88
  79.1 2.6 %copy-done.1 = f32[4,2,96,2048]{3,2,1,0:T(8,128)} copy-done((f32[4,2,96,2048]{3,2,1,0:T(8,128)}, f32[4,2,96,2048]{3,2,1,0:T(8,128)S(1)}, u32[]{:S(2)}) %copy-start.1) | copy-done | bytes 6291480
  81.7 1.4 fusion.15
  83.1 2.4 %collective-permute-start = (bf16[4,96,2048]{2,1,0:T(8,128)(2,1)}, bf16[4,96,2048]{2,1,0:T(8,128)(2,1)}, u32[]{:S(2)}, u32[]{:S(2)}) collective-permute-start(bf16[4,96,2048]{2,1,0:T(8,128)(2,1)} %fusion.15), channel_id=1, source_target_pairs={{0,4},{4,0},{8,12},{12,8},{16,20},{20,16},{24,28},{28,24},{1,5},{5... | collective-permute-start | bytes 4718600 | tf_op jit(solution)/shard_map/ppermute | solution.py:30
  85.5 3.6 %fusion.9 = bf16[384,2048]{1,0:T(8,128)(2,1)} fusion(bf16[384,768]{1,0:T(8,128)(2,1)} %get-tuple-element.9, bf16[1,768,2048]{2,1,0:T(8,128)(2,1)S(1)} %copy-done), kind=kOutput, calls=%fused_computation.13 | convolution fusion | flops 1208745984 | bytes 5308416 | tf_op jit(solution)/shard_map/dot_general | solution.py:93
  89.1 4.4 %all-to-all-start.1 = ((bf16[4,96,2048]{2,1,0:T(8,128)(2,1)}), bf16[4,96,2048]{2,1,0:T(8,128)(2,1)}, u32[]{:S(2)}, u32[]{:S(2)}) async-start(bf16[4,96,2048]{2,1,0:T(8,128)(2,1)} %bitcast.77), calls=%async_computation.1 | async-start | bytes 3145728 | tf_op jit(solution)/shard_map/all_to_all | solution.py:64
  93.5 42.9 %collective-permute-done = bf16[4,96,2048]{2,1,0:T(8,128)(2,1)} collective-permute-done((bf16[4,96,2048]{2,1,0:T(8,128)(2,1)}, bf16[4,96,2048]{2,1,0:T(8,128)(2,1)}, u32[]{:S(2)}, u32[]{:S(2)}) %collective-permute-start) | collective-permute-done | bytes 1572896 | tf_op jit(solution)/shard_map/ppermute | solution.py:30
  136.3 3.0 %bitcast_add_fusion = f32[4,96,2048]{2,1,0:T(8,128)S(1)} fusion(bf16[4,96,2048]{2,1,0:T(8,128)(2,1)} %collective-permute-done, f32[4,2,96,2048]{3,2,1,0:T(8,128)} %copy-done.1, s32[]{:T(128)S(6)} %select_n.65), kind=kLoop, calls=%fused_computation.6 | loop fusion | flops 1572864 | bytes 7864324 | tf_op jit(solution)/shard_map/add | solution.py:33
  139.4 1.7 copy-done.2
  141.1 1.0 fusion.17
  142.1 2.2 %collective-permute-start.1 = (bf16[2,96,2048]{2,1,0:T(8,128)(2,1)}, bf16[2,96,2048]{2,1,0:T(8,128)(2,1)}, u32[]{:S(2)}, u32[]{:S(2)}) collective-permute-start(bf16[2,96,2048]{2,1,0:T(8,128)(2,1)} %fusion.17), channel_id=1, source_target_pairs={{0,8},{4,12},{8,0},{12,4},{16,24},{20,28},{24,16},{28,20},{1,9},{5... | collective-permute-start | bytes 2359304 | tf_op jit(solution)/shard_map/ppermute | solution.py:30
  144.3 8.2 %fusion.12 = bf16[384,2048]{1,0:T(8,128)(2,1)} fusion(bf16[1,2048,1536]{2,1,0:T(8,128)(2,1)} %param.9, bf16[384,768]{1,0:T(8,128)(2,1)S(1)} %copy-done.11, bf16[384,768]{1,0:T(8,128)(2,1)S(1)} %copy-done.9), kind=kOutput, calls=%fused_computation.14 | convolution fusion | flops 2419064832 | bytes 9043968 | tf_op jit(solution)/shard_map/dot_general | solution.py:96
  152.5 0.0 all-to-all-done.1
  152.5 4.4 %all-to-all-start.3 = ((bf16[4,96,2048]{2,1,0:T(8,128)(2,1)}), bf16[4,96,2048]{2,1,0:T(8,128)(2,1)}, u32[]{:S(2)}, u32[]{:S(2)}) async-start(bf16[4,96,2048]{2,1,0:T(8,128)(2,1)} %bitcast.76), calls=%async_computation.3 | async-start | bytes 3145728 | tf_op jit(solution)/shard_map/all_to_all | solution.py:64
  156.9 2.1 convert_element_type.74
  159.0 0.7 fusion.21
  159.8 1.3 collective-permute-done.1
  161.1 1.8 bitcast_add_fusion.1
  162.9 1.1 copy-done.3
  164.1 0.8 dynamic-slice_convert_fusion.1
  164.9 3.3 %collective-permute-start.2 = (bf16[1,96,2048]{2,1,0:T(8,128)(2,1)}, bf16[1,96,2048]{2,1,0:T(8,128)(2,1)S(1)}, u32[]{:S(2)}, u32[]{:S(2)}) collective-permute-start(bf16[1,96,2048]{2,1,0:T(8,128)(2,1)} %dynamic-slice_convert_fusion.1), channel_id=1, source_target_pairs={{0,16},{4,20},{8,24},{12,28},{16,0},{20,4},{24,8},{28,12},{1,17},{... | collective-permute-start | bytes 1179656 | tf_op jit(solution)/shard_map/ppermute | solution.py:30
  168.2 3.3 %multiply_reduce_fusion = (f32[2,128]{1,0:T(2,128)}, bf16[128,2048]{1,0:T(8,128)(2,1)}) fusion(f32[128,2048]{1,0:T(8,128)S(1)} %copy-done.5, f32[2,128]{1,0:T(2,128)S(1)} %bitcast.83, bf16[384,2048,1]{1,0,2:T(8,128)(2,1)} %bitcast.10, s32[2,128]{1,0:T(2,128)S(1)} %select_reduce_fusion.2), kind=kOutput, calls=%fused_computation.17 | convolution fusion | flops 404586240 | bytes 3148800 | tf_op jit(solution)/shard_map/dot_general | solution.py:103
  171.5 5.5 %all-to-all-done.3 = bf16[4,96,2048]{2,1,0:T(8,128)(2,1)} async-done(((bf16[4,96,2048]{2,1,0:T(8,128)(2,1)}), bf16[4,96,2048]{2,1,0:T(8,128)(2,1)}, u32[]{:S(2)}, u32[]{:S(2)}) %all-to-all-start.3) | async-done | bytes 1572896 | tf_op jit(solution)/shard_map/all_to_all | solution.py:64
  177.0 2.8 %convolution_convert_fusion.2 = bf16[128,2048]{1,0:T(8,128)(2,1)} fusion(pred[128,384]{1,0:T(8,128)(4,1)} %fusion.21, bf16[384,2048]{1,0:T(8,128)(2,1)} %bitcast.14), kind=kOutput, calls=%fused_computation.16 | convolution fusion | flops 201588736 | bytes 2146304 | tf_op jit(solution)/shard_map/dot_general | solution.py:111
  179.8 25.5 %collective-permute-done.2 = bf16[1,96,2048]{2,1,0:T(8,128)(2,1)S(1)} collective-permute-done((bf16[1,96,2048]{2,1,0:T(8,128)(2,1)}, bf16[1,96,2048]{2,1,0:T(8,128)(2,1)S(1)}, u32[]{:S(2)}, u32[]{:S(2)}) %collective-permute-start.2) | collective-permute-done | bytes 393248 | tf_op jit(solution)/shard_map/ppermute | solution.py:30
  205.3 0.8 add_convert_fusion
  206.1 5.6 %reduce-scatter.2.cloned.1.call-done = bf16[1,256,1536]{2,1,0:T(8,128)(2,1)} async-done(((bf16[1,2048,1536]{2,1,0:T(8,128)(2,1)}), bf16[1,256,1536]{2,1,0:T(8,128)(2,1)}) %reduce-scatter.2.cloned.1.call-update) | async-done | bytes 786448 | tf_op jit(solution)/shard_map/reduce_scatter | solution.py:85
  (22 shorter events, 0.1 us)
Async XLA Ops:
  7.2 53.7 %copy-start = (bf16[1,768,2048]{2,1,0:T(8,128)(2,1)S(1)}, bf16[1,768,2048]{2,1,0:T(8,128)(2,1)}, u32[]{:S(2)}) copy-start(bf16[1,768,2048]{2,1,0:T(8,128)(2,1)} %param.10) | copy-start | bytes 9437188
  11.2 4.5 %copy-start.6 = (s32[128,2]{0,1:T(2,128)S(1)}, s32[128,2]{0,1:T(2,128)}, u32[]{:S(2)}) copy-start(s32[128,2]{0,1:T(2,128)} %param.7) | copy-start | bytes 3076
  11.2 4.5 %copy-start.7 = (f32[128,2]{0,1:T(2,128)S(1)}, f32[128,2]{0,1:T(2,128)}, u32[]{:S(2)}) copy-start(f32[128,2]{0,1:T(2,128)} %param.8) | copy-start | bytes 3076
  11.2 25.2 %all-to-all-start = ((bf16[4,96,2048]{2,1,0:T(8,128)(2,1)}), bf16[4,96,2048]{2,1,0:T(8,128)(2,1)}, u32[]{:S(2)}, u32[]{:S(2)}) async-start(bf16[4,96,2048]{2,1,0:T(8,128)(2,1)} %bitcast.74), calls=%async_computation | async-start | bytes 3145728 | tf_op jit(solution)/shard_map/all_to_all | solution.py:64
  36.4 24.5 %all-to-all-start.2 = ((bf16[4,96,2048]{2,1,0:T(8,128)(2,1)}), bf16[4,96,2048]{2,1,0:T(8,128)(2,1)}, u32[]{:S(2)}, u32[]{:S(2)}) async-start(bf16[4,96,2048]{2,1,0:T(8,128)(2,1)} %bitcast.73), calls=%async_computation.2 | async-start | bytes 3145728 | tf_op jit(solution)/shard_map/all_to_all | solution.py:64
  40.7 171.0 %reduce-scatter.2.cloned.1.call-start = ((), (), s32[]{:S(2)}) async-start(), calls=%async_computation.5 | async-start | bytes 7077888 | tf_op jit(solution)/shard_map/reduce_scatter | solution.py:85
  65.5 0.8 copy-start.8
  65.5 1.0 copy-start.10
  79.1 2.6 %copy-start.1 = (f32[4,2,96,2048]{3,2,1,0:T(8,128)}, f32[4,2,96,2048]{3,2,1,0:T(8,128)S(1)}, u32[]{:S(2)}) copy-start(f32[4,2,96,2048]{3,2,1,0:T(8,128)S(1)} %fusion.26) | copy-start | bytes 18874372
  83.1 53.2 %collective-permute-start = (bf16[4,96,2048]{2,1,0:T(8,128)(2,1)}, bf16[4,96,2048]{2,1,0:T(8,128)(2,1)}, u32[]{:S(2)}, u32[]{:S(2)}) collective-permute-start(bf16[4,96,2048]{2,1,0:T(8,128)(2,1)} %fusion.15), channel_id=1, source_target_pairs={{0,4},{4,0},{8,12},{12,8},{16,20},{20,16},{24,28},{28,24},{1,5},{5... | collective-permute-start | bytes 4718600 | tf_op jit(solution)/shard_map/ppermute | solution.py:30
  89.1 63.4 %all-to-all-start.1 = ((bf16[4,96,2048]{2,1,0:T(8,128)(2,1)}), bf16[4,96,2048]{2,1,0:T(8,128)(2,1)}, u32[]{:S(2)}, u32[]{:S(2)}) async-start(bf16[4,96,2048]{2,1,0:T(8,128)(2,1)} %bitcast.77), calls=%async_computation.1 | async-start | bytes 3145728 | tf_op jit(solution)/shard_map/all_to_all | solution.py:64
  139.4 1.7 copy-start.2
  139.4 4.9 %copy-start.9 = (bf16[384,768]{1,0:T(8,128)(2,1)S(1)}, bf16[384,768]{1,0:T(8,128)(2,1)}, u32[]{:S(2)}) copy-start(bf16[384,768]{1,0:T(8,128)(2,1)} %copy-done.8) | copy-start | bytes 1769476
  139.4 4.9 %copy-start.11 = (bf16[384,768]{1,0:T(8,128)(2,1)S(1)}, bf16[384,768]{1,0:T(8,128)(2,1)}, u32[]{:S(2)}) copy-start(bf16[384,768]{1,0:T(8,128)(2,1)} %copy-done.10) | copy-start | bytes 1769476
  142.1 19.0 %collective-permute-start.1 = (bf16[2,96,2048]{2,1,0:T(8,128)(2,1)}, bf16[2,96,2048]{2,1,0:T(8,128)(2,1)}, u32[]{:S(2)}, u32[]{:S(2)}) collective-permute-start(bf16[2,96,2048]{2,1,0:T(8,128)(2,1)} %fusion.17), channel_id=1, source_target_pairs={{0,8},{4,12},{8,0},{12,4},{16,24},{20,28},{24,16},{28,20},{1,9},{5... | collective-permute-start | bytes 2359304 | tf_op jit(solution)/shard_map/ppermute | solution.py:30
  152.5 24.5 %all-to-all-start.3 = ((bf16[4,96,2048]{2,1,0:T(8,128)(2,1)}), bf16[4,96,2048]{2,1,0:T(8,128)(2,1)}, u32[]{:S(2)}, u32[]{:S(2)}) async-start(bf16[4,96,2048]{2,1,0:T(8,128)(2,1)} %bitcast.76), calls=%async_computation.3 | async-start | bytes 3145728 | tf_op jit(solution)/shard_map/all_to_all | solution.py:64
  159.8 8.4 %copy-start.5 = (f32[128,2048]{1,0:T(8,128)S(1)}, f32[128,2048]{1,0:T(8,128)}, u32[]{:S(2)}) copy-start(f32[128,2048]{1,0:T(8,128)} %convert_element_type.74) | copy-start | bytes 3145732
  162.9 1.2 copy-start.3
  164.9 40.4 %collective-permute-start.2 = (bf16[1,96,2048]{2,1,0:T(8,128)(2,1)}, bf16[1,96,2048]{2,1,0:T(8,128)(2,1)S(1)}, u32[]{:S(2)}, u32[]{:S(2)}) collective-permute-start(bf16[1,96,2048]{2,1,0:T(8,128)(2,1)} %dynamic-slice_convert_fusion.1), channel_id=1, source_target_pairs={{0,16},{4,20},{8,24},{12,28},{16,0},{20,4},{24,8},{28,12},{1,17},{... | collective-permute-start | bytes 1179656 | tf_op jit(solution)/shard_map/ppermute | solution.py:30
  177.0 28.3 %copy-start.4 = (f32[2,96,2048]{2,1,0:T(8,128)S(1)}, f32[2,96,2048]{2,1,0:T(8,128)}, u32[]{:S(2)}) copy-start(f32[2,96,2048]{2,1,0:T(8,128)} %copy-done.3) | copy-start | bytes 4718596
Sparse Core Ops, SparseCore 0:
  73.6 138.0 reduce-scatter.1

commit v3 on v2

--- a/solution.py
+++ b/solution.py
@@ -77,15 +77,42 @@
             jnp.bfloat16
         )
     )
+    half = shards // 2
+    low = lax.axis_index("dp") % 2
+    swap = [(i, i ^ 1) for i in range(shards)]
+    block = model_width // shards
+
+    def columns(which):
+        return jnp.concatenate(
+            [
+                lax.dynamic_slice_in_dim(received, (2 * h + which) * block, block, axis=1)
+                for h in range(half)
+            ],
+            axis=1,
+        )
+
+    grad_rows, other_received = lax.optimization_barrier(
+        (grad_rows, lax.ppermute(columns(1 - low), "dp", swap))
+    )
     gate_up = jnp.dot(received, weight_in, preferred_element_type=jnp.float32)
     gate_part, up_part, hidden = swiglu_forward(gate_up, hidden_width)
     grad_hidden = jnp.dot(grad_rows, weight_out.T, preferred_element_type=jnp.float32)
     grad_gate_up = swiglu_backward(grad_hidden, gate_part, up_part)
-    grad_w_in = jnp.dot(received.T, grad_gate_up, preferred_element_type=jnp.float32)
+    grad_w_out = jnp.dot(hidden.T, grad_rows, preferred_element_type=jnp.float32)
+    other_grad, grad_w_out = lax.optimization_barrier(
+        (lax.ppermute(grad_gate_up, "dp", swap), grad_w_out)
+    )
+    grad_w_in = jnp.dot(columns(low).T, grad_gate_up, preferred_element_type=jnp.float32)
+    grad_w_in = grad_w_in + jnp.dot(
+        other_received.T, other_grad, preferred_element_type=jnp.float32
+    )
     shard_in = lax.psum_scatter(
-        grad_w_in.astype(jnp.bfloat16)[None], "dp", scatter_dimension=1, tiled=True
+        grad_w_in.astype(jnp.bfloat16)[None],
+        "dp",
+        scatter_dimension=1,
+        axis_index_groups=[[2 * h + b for h in range(half)] for b in range(2)],
+        tiled=True,
     )
-    grad_w_out = jnp.dot(hidden.T, grad_rows, preferred_element_type=jnp.float32)
     shard_out = halving_sum(
         grad_w_out.reshape(shards, hidden_width // shards, model_width), "dp"
     )[None]

time: 219 us -> 210 us (0.959)
  waiting for transfers between devices: 111 us -> 99.7 us
    ppermute x0 -> x2, waiting for transfers between devices: none -> 22.1 us  [the longest x1 18.2 us: per_device(): lax.ppermute(grad_gate_up, 'dp', swap)]
    ppermute x3, waiting for transfers between devices: 69.7 us -> 52.7 us  [halving_sum(): lax.ppermute(send.astype(jnp.bfloat16), axis, [(i, i ^ bit) for i in rang...]
    all_to_all x4, waiting for transfers between devices: 36 us -> 24.8 us  [exchange(): lax.all_to_all(rows.reshape(groups, capacity, model_width), 'expert', spl...]
    reduce_scatter x1, waiting for transfers between devices: 5.62 us -> 0.01 us  [per_device(): lax.psum_scatter(grad_w_in.astype(jnp.bfloat16)[None], 'dp', scatter_dime...]
    ppermute x0 -> x2, starting transfers between devices: none -> 4.17 us  [the longest x1 2.36 us: per_device(): lax.ppermute(columns(1 - low), 'dp', swap)]
    unnamed x24 -> x28, local copies, waits for them, and re-layouts: 6.51 us -> 2.81 us
    dot_general x1, matrix products: 3.39 us -> 5.9 us  [per_device(): jnp.dot(hidden.T, grad_rows, preferred_element_type=jnp.float32)]
    dynamic_slice x0 -> x1, local copies, waits for them, and re-layouts: none -> 2.34 us  [columns(): lax.dynamic_slice_in_dim(received, (2 * h + which) * block, block, axis=1)]
  transfers between devices with their start and end apart: 8 -> 10, of which waited for: 7 -> 7; matrix products, arithmetic and copies ran while one was open for 21% -> 25% of each run, Pallas kernels for 0% -> 0%
where the time goes in v3:
time: 210 us; the launch traced here: 209 us
  waiting for transfers between devices  99.7 us (47%)
  matrix products  46.9 us (22%)
  starting transfers between devices  27.6 us (13%)
  between operations  14.3 us (7%)
  other arithmetic  10.6 us (5%)
  local copies, waits for them, and re-layouts  10.4 us (5%)
    ppermute x3, waiting for transfers between devices, halving_sum(): lax.ppermute(send.astype(jnp.bfloat16), axis, [(i, i ^ bit) for i in rang...  52.7 us
    all_to_all x4, waiting for transfers between devices, exchange(): lax.all_to_all(rows.reshape(groups, capacity, model_width), 'expert', spl...  24.8 us
    ppermute x1, waiting for transfers between devices, per_device(): lax.ppermute(grad_gate_up, 'dp', swap)  18.2 us
    all_to_all x4, starting transfers between devices, exchange(): lax.all_to_all(rows.reshape(groups, capacity, model_width), 'expert', spl...  17.7 us
    dot_general x1, matrix products, per_device(): jnp.dot(grad_gate_up, weight_in.T, preferred_element_type=jnp.float32)  8.04 us
    dot_general x1, matrix products, per_device(): gate_up = jnp.dot(received, weight_in, preferred_element_type=jnp.float32)  7.27 us
    dot_general x1, matrix products, per_device(): jnp.dot(hidden.T, grad_rows, preferred_element_type=jnp.float32)  5.9 us
    ppermute x3, starting transfers between devices, halving_sum(): lax.ppermute(send.astype(jnp.bfloat16), axis, [(i, i ^ bit) for i in rang...  5.63 us
  transfers between devices with their start and end apart: 10, of which 7 were waited for; matrix products, arithmetic and copies ran while one was open for 25% of the time, Pallas kernels for 0%

profile of v3, /device:TPU:0, one launch (start us, length us, event | category | flops | bytes accessed | tf_op | source)
XLA Modules:
  0.0 209.5 jit_solution(17344809567000300327)
XLA Ops:
  7.2 0.8 fusion.31
  8.0 0.1 eq.88
  8.1 0.1 broadcast_add_fusion
  8.2 0.2 bitcast_compare_fusion
  8.4 2.8 %convolution_convert_fusion = bf16[384,2048]{1,0:T(8,128)(2,1)} fusion(pred[384,128]{1,0:T(32,128)(4,1)S(1)} %bitcast_compare_fusion, bf16[128,2048]{1,0:T(8,128)(2,1)} %param.6), kind=kOutput, calls=%fused_computation.15 | convolution fusion | flops 202113024 | bytes 2146304 | tf_op jit(solution)/shard_map/dot_general | solution.py:73
  11.2 4.5 %all-to-all-start = ((bf16[4,96,2048]{2,1,0:T(8,128)(2,1)}), bf16[4,96,2048]{2,1,0:T(8,128)(2,1)}, u32[]{:S(2)}, u32[]{:S(2)}) async-start(bf16[4,96,2048]{2,1,0:T(8,128)(2,1)} %bitcast.72), calls=%async_computation | async-start | bytes 3145728 | tf_op jit(solution)/shard_map/all_to_all | solution.py:64
  15.7 0.1 select_reduce_fusion
  15.8 0.1 mul.86
  15.9 2.8 %multiply_convert_fusion = bf16[384,2048]{1,0:T(8,128)(2,1)} fusion(pred[384,128]{1,0:T(32,128)(4,1)S(1)} %bitcast_compare_fusion, bf16[128,2048]{1,0:T(8,128)(2,1)} %param.11, f32[384]{0:T(512)S(1)} %mul.86), kind=kOutput, calls=%fused_computation.12 | convolution fusion | flops 202899456 | bytes 2147840 | tf_op jit(solution)/shard_map/dot_general | solution.py:76
  18.7 17.7 %all-to-all-done = bf16[4,96,2048]{2,1,0:T(8,128)(2,1)} async-done(((bf16[4,96,2048]{2,1,0:T(8,128)(2,1)}), bf16[4,96,2048]{2,1,0:T(8,128)(2,1)}, u32[]{:S(2)}, u32[]{:S(2)}) %all-to-all-start) | async-done | bytes 1572896 | tf_op jit(solution)/shard_map/all_to_all | solution.py:64
  36.4 4.4 %all-to-all-start.2 = ((bf16[4,96,2048]{2,1,0:T(8,128)(2,1)}), bf16[4,96,2048]{2,1,0:T(8,128)(2,1)}, u32[]{:S(2)}, u32[]{:S(2)}) async-start(bf16[4,96,2048]{2,1,0:T(8,128)(2,1)} %bitcast.71), calls=%async_computation.2 | async-start | bytes 3145728 | tf_op jit(solution)/shard_map/all_to_all | solution.py:64
  40.8 0.0 reduce-scatter.2.cloned.1.call-start
  40.9 2.3 %constant_dynamic-slice_fusion.3 = (bf16[384,256]{1,0:T(8,128)(2,1)S(1)}, bf16[384,256]{1,0:T(8,128)(2,1)S(1)}, bf16[384,256]{1,0:T(8,128)(2,1)}, bf16[384,256]{...) fusion(bf16[384,2048]{1,0:T(8,128)(2,1)} %bitcast.5, ...), kind=kLoop, calls=%fused_computation.58 | loop fusion | bytes 3145760 | tf_op jit(solution)/shard_map/dynamic_slice | solution.py:88
  43.2 1.0 pad_maximum_fusion.1
  44.2 2.4 %collective-permute-start = (bf16[384,1024]{1,0:T(8,128)(2,1)}, bf16[384,1024]{1,0:T(8,128)(2,1)}, u32[]{:S(2)}, u32[]{:S(2)}) collective-permute-start(bf16[384,1024]{1,0:T(8,128)(2,1)} %pad_maximum_fusion.1), channel_id=1, source_target_pairs={{0,4},{4,0},{8,12},{12,8},{16,20},{20,16},{24,28},{28,24},{1,5},{5... | collective-permute-start | bytes 2359304 | tf_op jit(solution)/shard_map/ppermute | solution.py:95
  46.5 7.3 %fusion.2 = f32[384,1536]{1,0:T(8,128)} fusion(bf16[384,2048]{1,0:T(8,128)(2,1)} %bitcast.5, bf16[1,2048,1536]{2,1,0:T(8,128)(2,1)} %param.9), kind=kOutput, calls=%fused_computation.2 | convolution fusion | flops 2415919104 | bytes 10223616 | tf_op jit(solution)/shard_map/dot_general | solution.py:97
  53.8 7.1 %all-to-all-done.2 = bf16[4,96,2048]{2,1,0:T(8,128)(2,1)} async-done(((bf16[4,96,2048]{2,1,0:T(8,128)(2,1)}), bf16[4,96,2048]{2,1,0:T(8,128)(2,1)}, u32[]{:S(2)}, u32[]{:S(2)}) %all-to-all-start.2) | async-done | bytes 1572896 | tf_op jit(solution)/shard_map/all_to_all | solution.py:64
  60.9 4.0 %collective-permute-done = bf16[384,1024]{1,0:T(8,128)(2,1)} collective-permute-done((bf16[384,1024]{1,0:T(8,128)(2,1)}, bf16[384,1024]{1,0:T(8,128)(2,1)}, u32[]{:S(2)}, u32[]{:S(2)}) %collective-permute-start) | collective-permute-done | bytes 786464 | tf_op jit(solution)/shard_map/ppermute | solution.py:95
  64.9 3.8 %multiply_convert_fusion.2 = (bf16[384,768]{1,0:T(8,128)(2,1)S(1)}, bf16[384,768]{1,0:T(8,128)(2,1)S(1)}, bf16[384,768]{1,0:T(8,128)(2,1)S(1)}) fusion(f32[384,1536]{1,0:T(8,128)} %fusion.2, bf16[384,2048]{1,0:T(8,128)(2,1)} %bitcast.12, bf16[1,768,2048]{2,1,0:T(8,128)(2,1)S(1)} %copy-done), kind=kOutput, calls=%fused_computation.24 | convolution fusion | flops 1212383232 | bytes 8847360 | tf_op jit(solution)/shard_map/dot_general | solution.py:99
  68.8 0.1 pad_maximum_fusion
  68.9 1.8 collective-permute-start.1
  70.7 1.8 fusion.18
  72.5 5.9 %fusion.33 = f32[768,2048]{1,0:T(8,128)} fusion(bf16[384,768]{1,0:T(8,128)(2,1)S(1)} %get-tuple-element.17, bf16[384,2048]{1,0:T(8,128)(2,1)} %bitcast.12), kind=kOutput, calls=%fused_computation.67 | convolution fusion | flops 1207959552 | bytes 8454144 | tf_op jit(solution)/shard_map/dot_general | solution.py:101
  78.4 18.2 %collective-permute-done.1 = bf16[384,1536]{1,0:T(8,128)(2,1)S(1)} collective-permute-done((bf16[384,1536]{1,0:T(8,128)(2,1)S(1)}, bf16[384,1536]{1,0:T(8,128)(2,1)S(1)}, u32[]{:S(2)}, u32[]{:S(2)}) %collective-permute-start.1) | collective-permute-done | bytes 1179680 | tf_op jit(solution)/shard_map/ppermute | solution.py:103
  96.6 4.7 %fusion.4 = bf16[1,1024,1536]{2,1,0:T(8,128)(2,1)} fusion(f32[1024,1536]{1,0:T(8,128)S(1)} %fusion.18, bf16[384,1024]{1,0:T(8,128)(2,1)} %collective-permute-done, bf16[384,1536]{1,0:T(8,128)(2,1)S(1)} %collective-permute-done.1), kind=kOutput, calls=%fused_computation.5 | convolution fusion | flops 1211105280 | bytes 11403264 | tf_op jit(solution)/shard_map/dot_general | solution.py:106
  101.3 0.0 reduce-scatter.2.cloned.1.call-update
  101.3 3.3 %fusion.15 = bf16[4,96,2048]{2,1,0:T(8,128)(2,1)} fusion(f32[4,2,96,2048]{3,2,1,0:T(8,128)} %bitcast.67, s32[]{:T(128)S(6)} %select_n.100), kind=kLoop, calls=%fused_computation.19 | loop fusion | bytes 3145732 | tf_op jit(solution)/shard_map/convert_element_type | solution.py:31
  104.6 1.5 collective-permute-start.2
  106.1 3.6 %fusion.9 = bf16[384,2048]{1,0:T(8,128)(2,1)} fusion(bf16[384,768]{1,0:T(8,128)(2,1)} %copy-done.11, bf16[1,768,2048]{2,1,0:T(8,128)(2,1)S(1)} %copy-done), kind=kOutput, calls=%fused_computation.13 | convolution fusion | flops 1208745984 | bytes 5308416 | tf_op jit(solution)/shard_map/dot_general | solution.py:120
  109.7 4.5 %all-to-all-start.1 = ((bf16[4,96,2048]{2,1,0:T(8,128)(2,1)}), bf16[4,96,2048]{2,1,0:T(8,128)(2,1)}, u32[]{:S(2)}, u32[]{:S(2)}) async-start(bf16[4,96,2048]{2,1,0:T(8,128)(2,1)} %bitcast.74), calls=%async_computation.1 | async-start | bytes 3145728 | tf_op jit(solution)/shard_map/all_to_all | solution.py:64
  114.2 25.9 %collective-permute-done.2 = bf16[4,96,2048]{2,1,0:T(8,128)(2,1)} collective-permute-done((bf16[4,96,2048]{2,1,0:T(8,128)(2,1)}, bf16[4,96,2048]{2,1,0:T(8,128)(2,1)}, u32[]{:S(2)}, u32[]{:S(2)}) %collective-permute-start.2) | collective-permute-done | bytes 1572896 | tf_op jit(solution)/shard_map/ppermute | solution.py:30
  140.1 2.9 %bitcast_add_fusion = f32[4,96,2048]{2,1,0:T(8,128)S(1)} fusion(bf16[4,96,2048]{2,1,0:T(8,128)(2,1)} %collective-permute-done.2, f32[4,2,96,2048]{3,2,1,0:T(8,128)} %bitcast.68, s32[]{:T(128)S(6)} %select_n.99), kind=kLoop, calls=%fused_computation.7 | loop fusion | flops 1572864 | bytes 7864324 | tf_op jit(solution)/shard_map/add | solution.py:33
  143.0 1.6 copy-done.1
  144.6 1.0 fusion.17
  145.6 1.3 collective-permute-start.3
  146.9 8.0 %fusion.12 = bf16[384,2048]{1,0:T(8,128)(2,1)} fusion(bf16[1,2048,1536]{2,1,0:T(8,128)(2,1)} %param.9, bf16[384,768]{1,0:T(8,128)(2,1)S(1)} %copy-done.7, bf16[384,768]{1,0:T(8,128)(2,1)S(1)} %copy-done.5), kind=kOutput, calls=%fused_computation.14 | convolution fusion | flops 2419064832 | bytes 9043968 | tf_op jit(solution)/shard_map/dot_general | solution.py:123
  155.0 4.4 %all-to-all-start.3 = ((bf16[4,96,2048]{2,1,0:T(8,128)(2,1)}), bf16[4,96,2048]{2,1,0:T(8,128)(2,1)}, u32[]{:S(2)}, u32[]{:S(2)}) async-start(bf16[4,96,2048]{2,1,0:T(8,128)(2,1)} %bitcast.73), calls=%async_computation.3 | async-start | bytes 3145728 | tf_op jit(solution)/shard_map/all_to_all | solution.py:64
  159.4 2.1 %convert_element_type.74 = f32[128,2048]{1,0:T(8,128)} convert(bf16[128,2048]{1,0:T(8,128)(2,1)} %param.11) | non-fusion elementwise | flops 262144 | bytes 1572864 | tf_op jit(solution)/shard_map/convert_element_type | solution.py:135
  161.5 0.7 fusion.29
  162.3 15.9 %collective-permute-done.3 = bf16[2,96,2048]{2,1,0:T(8,128)(2,1)} collective-permute-done((bf16[2,96,2048]{2,1,0:T(8,128)(2,1)}, bf16[2,96,2048]{2,1,0:T(8,128)(2,1)}, u32[]{:S(2)}, u32[]{:S(2)}) %collective-permute-start.3) | collective-permute-done | bytes 786464 | tf_op jit(solution)/shard_map/ppermute | solution.py:30
  178.1 1.8 bitcast_add_fusion.1
  180.0 1.1 copy-done.2
  181.1 0.8 dynamic-slice_convert_fusion.1
  181.9 2.8 %collective-permute-start.4 = (bf16[1,96,2048]{2,1,0:T(8,128)(2,1)}, bf16[1,96,2048]{2,1,0:T(8,128)(2,1)S(1)}, u32[]{:S(2)}, u32[]{:S(2)}) collective-permute-start(bf16[1,96,2048]{2,1,0:T(8,128)(2,1)} %dynamic-slice_convert_fusion.1), channel_id=1, source_target_pairs={{0,16},{4,20},{8,24},{12,28},{16,0},{20,4},{24,8},{28,12},{1,17},{... | collective-permute-start | bytes 1179656 | tf_op jit(solution)/shard_map/ppermute | solution.py:30
  184.7 3.3 %multiply_reduce_fusion = (f32[2,128]{1,0:T(2,128)}, bf16[128,2048]{1,0:T(8,128)(2,1)}) fusion(f32[128,2048]{1,0:T(8,128)S(1)} %copy-done.8, f32[2,128]{1,0:T(2,128)S(1)} %bitcast.79, bf16[384,2048,1]{1,0,2:T(8,128)(2,1)} %bitcast.10, s32[2,128]{1,0:T(2,128)S(1)} %select_reduce_fusion.2), kind=kOutput, calls=%fused_computation.17 | convolution fusion | flops 404586240 | bytes 3148800 | tf_op jit(solution)/shard_map/dot_general | solution.py:130
  188.0 2.8 %convolution_convert_fusion.1 = bf16[128,2048]{1,0:T(8,128)(2,1)} fusion(pred[128,384]{1,0:T(8,128)(4,1)} %fusion.29, bf16[384,2048]{1,0:T(8,128)(2,1)} %bitcast.14), kind=kOutput, calls=%fused_computation.16 | convolution fusion | flops 201588736 | bytes 2146304 | tf_op jit(solution)/shard_map/dot_general | solution.py:138
  190.8 11.0 %collective-permute-done.4 = bf16[1,96,2048]{2,1,0:T(8,128)(2,1)S(1)} collective-permute-done((bf16[1,96,2048]{2,1,0:T(8,128)(2,1)}, bf16[1,96,2048]{2,1,0:T(8,128)(2,1)S(1)}, u32[]{:S(2)}, u32[]{:S(2)}) %collective-permute-start.4) | collective-permute-done | bytes 393248 | tf_op jit(solution)/shard_map/ppermute | solution.py:30
  201.8 0.8 add_convert_fusion.1
  (33 shorter events, 0.1 us)
Async XLA Ops:
  7.2 57.7 %copy-start = (bf16[1,768,2048]{2,1,0:T(8,128)(2,1)S(1)}, bf16[1,768,2048]{2,1,0:T(8,128)(2,1)}, u32[]{:S(2)}) copy-start(bf16[1,768,2048]{2,1,0:T(8,128)(2,1)} %param.10) | copy-start | bytes 9437188
  11.2 4.5 %copy-start.12 = (s32[128,2]{0,1:T(2,128)S(1)}, s32[128,2]{0,1:T(2,128)}, u32[]{:S(2)}) copy-start(s32[128,2]{0,1:T(2,128)} %param.7) | copy-start | bytes 3076
  11.2 4.5 %copy-start.13 = (f32[128,2]{0,1:T(2,128)S(1)}, f32[128,2]{0,1:T(2,128)}, u32[]{:S(2)}) copy-start(f32[128,2]{0,1:T(2,128)} %param.8) | copy-start | bytes 3076
  11.2 25.2 %all-to-all-start = ((bf16[4,96,2048]{2,1,0:T(8,128)(2,1)}), bf16[4,96,2048]{2,1,0:T(8,128)(2,1)}, u32[]{:S(2)}, u32[]{:S(2)}) async-start(bf16[4,96,2048]{2,1,0:T(8,128)(2,1)} %bitcast.72), calls=%async_computation | async-start | bytes 3145728 | tf_op jit(solution)/shard_map/all_to_all | solution.py:64
  36.4 24.5 %all-to-all-start.2 = ((bf16[4,96,2048]{2,1,0:T(8,128)(2,1)}), bf16[4,96,2048]{2,1,0:T(8,128)(2,1)}, u32[]{:S(2)}, u32[]{:S(2)}) async-start(bf16[4,96,2048]{2,1,0:T(8,128)(2,1)} %bitcast.71), calls=%async_computation.2 | async-start | bytes 3145728 | tf_op jit(solution)/shard_map/all_to_all | solution.py:64
  40.8 161.9 %reduce-scatter.2.cloned.1.call-start = ((), (), s32[]{:S(2)}) async-start(), calls=%async_computation.5 | async-start | bytes 3932160 | tf_op jit(solution)/shard_map/reduce_scatter | solution.py:109
  44.2 20.7 %collective-permute-start = (bf16[384,1024]{1,0:T(8,128)(2,1)}, bf16[384,1024]{1,0:T(8,128)(2,1)}, u32[]{:S(2)}, u32[]{:S(2)}) collective-permute-start(bf16[384,1024]{1,0:T(8,128)(2,1)} %pad_maximum_fusion.1), channel_id=1, source_target_pairs={{0,4},{4,0},{8,12},{12,8},{16,20},{20,16},{24,28},{28,24},{1,5},{5... | collective-permute-start | bytes 2359304 | tf_op jit(solution)/shard_map/ppermute | solution.py:95
  68.7 3.8 %copy-start.4 = (bf16[384,768]{1,0:T(8,128)(2,1)}, bf16[384,768]{1,0:T(8,128)(2,1)S(1)}, u32[]{:S(2)}) copy-start(bf16[384,768]{1,0:T(8,128)(2,1)S(1)} %get-tuple-element.15) | copy-start | bytes 1769476
  68.7 3.8 %copy-start.6 = (bf16[384,768]{1,0:T(8,128)(2,1)}, bf16[384,768]{1,0:T(8,128)(2,1)S(1)}, u32[]{:S(2)}) copy-start(bf16[384,768]{1,0:T(8,128)(2,1)S(1)} %get-tuple-element.16) | copy-start | bytes 1769476
  68.7 3.8 %copy-start.11 = (bf16[384,768]{1,0:T(8,128)(2,1)}, bf16[384,768]{1,0:T(8,128)(2,1)S(1)}, u32[]{:S(2)}) copy-start(bf16[384,768]{1,0:T(8,128)(2,1)S(1)} %get-tuple-element.17) | copy-start | bytes 1769476
  68.8 1.9 copy-start.9
  68.8 1.9 copy-start.10
  68.9 27.7 %collective-permute-start.1 = (bf16[384,1536]{1,0:T(8,128)(2,1)S(1)}, bf16[384,1536]{1,0:T(8,128)(2,1)S(1)}, u32[]{:S(2)}, u32[]{:S(2)}) collective-permute-start(bf16[384,1536]{1,0:T(8,128)(2,1)S(1)} %pad_maximum_fusion), channel_id=1, source_target_pairs={{0,4},{4,0},{8,12},{12,8},{16,20},{20,16},{24,28},{28,24},{1,5},{5... | collective-permute-start | bytes 3538952 | tf_op jit(solution)/shard_map/ppermute | solution.py:103
  104.6 35.5 %collective-permute-start.2 = (bf16[4,96,2048]{2,1,0:T(8,128)(2,1)}, bf16[4,96,2048]{2,1,0:T(8,128)(2,1)}, u32[]{:S(2)}, u32[]{:S(2)}) collective-permute-start(bf16[4,96,2048]{2,1,0:T(8,128)(2,1)} %fusion.15), channel_id=1, source_target_pairs={{0,4},{4,0},{8,12},{12,8},{16,20},{20,16},{24,28},{28,24},{1,5},{5... | collective-permute-start | bytes 4718600 | tf_op jit(solution)/shard_map/ppermute | solution.py:30
  109.7 45.3 %all-to-all-start.1 = ((bf16[4,96,2048]{2,1,0:T(8,128)(2,1)}), bf16[4,96,2048]{2,1,0:T(8,128)(2,1)}, u32[]{:S(2)}, u32[]{:S(2)}) async-start(bf16[4,96,2048]{2,1,0:T(8,128)(2,1)} %bitcast.74), calls=%async_computation.1 | async-start | bytes 3145728 | tf_op jit(solution)/shard_map/all_to_all | solution.py:64
  143.0 1.6 copy-start.1
  143.0 4.0 %copy-start.5 = (bf16[384,768]{1,0:T(8,128)(2,1)S(1)}, bf16[384,768]{1,0:T(8,128)(2,1)}, u32[]{:S(2)}) copy-start(bf16[384,768]{1,0:T(8,128)(2,1)} %copy-done.4) | copy-start | bytes 1769476
  143.0 3.9 %copy-start.7 = (bf16[384,768]{1,0:T(8,128)(2,1)S(1)}, bf16[384,768]{1,0:T(8,128)(2,1)}, u32[]{:S(2)}) copy-start(bf16[384,768]{1,0:T(8,128)(2,1)} %copy-done.6) | copy-start | bytes 1769476
  145.6 32.5 %collective-permute-start.3 = (bf16[2,96,2048]{2,1,0:T(8,128)(2,1)}, bf16[2,96,2048]{2,1,0:T(8,128)(2,1)}, u32[]{:S(2)}, u32[]{:S(2)}) collective-permute-start(bf16[2,96,2048]{2,1,0:T(8,128)(2,1)} %fusion.17), channel_id=1, source_target_pairs={{0,8},{4,12},{8,0},{12,4},{16,24},{20,28},{24,16},{28,20},{1,9},{5... | collective-permute-start | bytes 2359304 | tf_op jit(solution)/shard_map/ppermute | solution.py:30
  155.0 33.1 %all-to-all-start.3 = ((bf16[4,96,2048]{2,1,0:T(8,128)(2,1)}), bf16[4,96,2048]{2,1,0:T(8,128)(2,1)}, u32[]{:S(2)}, u32[]{:S(2)}) async-start(bf16[4,96,2048]{2,1,0:T(8,128)(2,1)} %bitcast.73), calls=%async_computation.3 | async-start | bytes 3145728 | tf_op jit(solution)/shard_map/all_to_all | solution.py:64
  162.3 22.5 %copy-start.8 = (f32[128,2048]{1,0:T(8,128)S(1)}, f32[128,2048]{1,0:T(8,128)}, u32[]{:S(2)}) copy-start(f32[128,2048]{1,0:T(8,128)} %convert_element_type.74) | copy-start | bytes 3145732
  180.0 1.2 copy-start.2
  181.9 19.9 %collective-permute-start.4 = (bf16[1,96,2048]{2,1,0:T(8,128)(2,1)}, bf16[1,96,2048]{2,1,0:T(8,128)(2,1)S(1)}, u32[]{:S(2)}, u32[]{:S(2)}) collective-permute-start(bf16[1,96,2048]{2,1,0:T(8,128)(2,1)} %dynamic-slice_convert_fusion.1), channel_id=1, source_target_pairs={{0,16},{4,20},{8,24},{12,28},{16,0},{20,4},{24,8},{28,12},{1,17},{... | collective-permute-start | bytes 1179656 | tf_op jit(solution)/shard_map/ppermute | solution.py:30
  188.0 13.8 %copy-start.3 = (f32[2,96,2048]{2,1,0:T(8,128)S(1)}, f32[2,96,2048]{2,1,0:T(8,128)}, u32[]{:S(2)}) copy-start(f32[2,96,2048]{2,1,0:T(8,128)} %copy-done.2) | copy-start | bytes 4718596
Sparse Core Ops, SparseCore 0:
  101.4 73.7 reduce-scatter.1

commit v4 on v3

--- a/solution.py
+++ b/solution.py
@@ -18,21 +18,27 @@
     return jnp.concatenate([grad_gate, grad_up], axis=1).astype(jnp.bfloat16)
 
 
-def halving_sum(parts, axis):
+def halving_sum(parts, axis, beside):
     count = lax.axis_size(axis)
     me = lax.axis_index(axis)
-    bit = 1
-    while bit < count:
+    bits = [1 << i for i in range(count.bit_length() - 1)]
+    left = list(bits)
+    for bit in bits[1:2] + bits[:1] + bits[2:]:
         mine = (me // bit) % 2
-        pairs = parts.reshape((parts.shape[0] // 2, 2) + parts.shape[1:])
-        keep = lax.dynamic_index_in_dim(pairs, mine, axis=1, keepdims=False)
-        send = lax.dynamic_index_in_dim(pairs, 1 - mine, axis=1, keepdims=False)
-        came = lax.ppermute(
-            send.astype(jnp.bfloat16), axis, [(i, i ^ bit) for i in range(count)]
-        )
-        parts = keep.astype(jnp.float32) + came.astype(jnp.float32)
-        bit *= 2
-    return parts[0].astype(jnp.bfloat16)
+        below = 1 << left.index(bit)
+
+        def side(x, which):
+            x = x.reshape((x.shape[0] // (2 * below), 2, below) + x.shape[1:])
+            x = lax.dynamic_index_in_dim(x, which, axis=1, keepdims=False)
+            return x.reshape((x.shape[0] * below,) + x.shape[2:])
+
+        send = side(parts, 1 - mine).astype(jnp.bfloat16)
+        if len(left) == len(bits):
+            send, beside = lax.optimization_barrier((send, beside))
+        came = lax.ppermute(send, axis, [(i, i ^ bit) for i in range(count)])
+        parts = side(parts, mine).astype(jnp.float32) + came.astype(jnp.float32)
+        left.remove(bit)
+    return parts[0].astype(jnp.bfloat16), beside
 
 
 def per_device(tokens, expert_ids, gates, w_in, w_out, out_grad):
@@ -99,9 +105,12 @@
     grad_hidden = jnp.dot(grad_rows, weight_out.T, preferred_element_type=jnp.float32)
     grad_gate_up = swiglu_backward(grad_hidden, gate_part, up_part)
     grad_w_out = jnp.dot(hidden.T, grad_rows, preferred_element_type=jnp.float32)
-    other_grad, grad_w_out = lax.optimization_barrier(
-        (lax.ppermute(grad_gate_up, "dp", swap), grad_w_out)
+    by_shard = (shards, hidden_width // shards, model_width)
+    other_gate = lax.ppermute(grad_gate_up[:, :hidden_width], "dp", swap)
+    shard_out, up_half = halving_sum(
+        grad_w_out.reshape(by_shard), "dp", grad_gate_up[:, hidden_width:]
     )
+    other_grad = jnp.concatenate([other_gate, lax.ppermute(up_half, "dp", swap)], axis=1)
     grad_w_in = jnp.dot(columns(low).T, grad_gate_up, preferred_element_type=jnp.float32)
     grad_w_in = grad_w_in + jnp.dot(
         other_received.T, other_grad, preferred_element_type=jnp.float32
@@ -113,9 +122,6 @@
         axis_index_groups=[[2 * h + b for h in range(half)] for b in range(2)],
         tiled=True,
     )
-    shard_out = halving_sum(
-        grad_w_out.reshape(shards, hidden_width // shards, model_width), "dp"
-    )[None]
     returned = exchange(
         jnp.dot(hidden, weight_out, preferred_element_type=jnp.float32).astype(jnp.bfloat16)
     )
@@ -138,7 +144,7 @@
     token_grad = jnp.dot(
         jnp.any(home, axis=0).astype(jnp.bfloat16), grad_back, preferred_element_type=jnp.float32
     ).astype(jnp.bfloat16)
-    return (mixed, token_grad, gate_grad, shard_in, shard_out)
+    return (mixed, token_grad, gate_grad, shard_in, shard_out[None])
 
 
 def solution(mesh):

time: 210 us -> 242 us (1.15)
  waiting for transfers between devices: 99.7 us -> 141 us
  matrix products: 46.9 us -> 40.9 us
  starting transfers between devices: 27.6 us -> 23.8 us
    ppermute x4 -> x5, waiting for transfers between devices: 70.9 us -> 104 us  [the longest x3 79.9 us: halving_sum(): came = lax.ppermute(send, axis, [(i, i ^ bit) for i in range(count)])]
    all_to_all x4, waiting for transfers between devices: 24.8 us -> 33.7 us  [exchange(): lax.all_to_all(rows.reshape(groups, capacity, model_width), 'expert', spl...]
    dot_general x1, matrix products: 8.04 us -> 3.8 us  [per_device(): jnp.dot(grad_gate_up, weight_in.T, preferred_element_type=jnp.float32)]
    ppermute x4 -> x5, starting transfers between devices: 7.44 us -> 3.66 us  [the longest x1 1.75 us: per_device(): lax.ppermute(up_half, 'dp', swap)]
  transfers between devices with their start and end apart: 10 -> 11, of which waited for: 7 -> 9; matrix products, arithmetic and copies ran while one was open for 25% -> 17% of each run, Pallas kernels for 0% -> 0%
where the time goes in v4:
time: 242 us; the launch traced here: 241 us
  waiting for transfers between devices  141 us (58%)
  matrix products  40.9 us (17%)
  starting transfers between devices  23.8 us (10%)
  between operations  14.4 us (6%)
  local copies, waits for them, and re-layouts  11 us (5%)
  other arithmetic  9.78 us (4%)
    ppermute x3, waiting for transfers between devices, halving_sum(): came = lax.ppermute(send, axis, [(i, i ^ bit) for i in range(count)])  79.9 us
    all_to_all x4, waiting for transfers between devices, exchange(): lax.all_to_all(rows.reshape(groups, capacity, model_width), 'expert', spl...  33.7 us
    all_to_all x4, starting transfers between devices, exchange(): lax.all_to_all(rows.reshape(groups, capacity, model_width), 'expert', spl...  17.8 us
    ppermute x1, waiting for transfers between devices, per_device(): lax.ppermute(up_half, 'dp', swap)  12.3 us
    ppermute x1, waiting for transfers between devices, per_device(): other_gate = lax.ppermute(grad_gate_up[:, :hidden_width], 'dp', swap)  11.4 us
    dot_general x1, matrix products, per_device(): gate_up = jnp.dot(received, weight_in, preferred_element_type=jnp.float32)  7.31 us
  transfers between devices with their start and end apart: 11, of which 9 were waited for; matrix products, arithmetic and copies ran while one was open for 17% of the time, Pallas kernels for 0%

profile of v4, /device:TPU:0, one launch (start us, length us, event | category | flops | bytes accessed | tf_op | source)
XLA Modules:
  0.0 241.2 jit_solution(2217477327462793304)
XLA Ops:
  7.2 0.8 fusion.33
  8.0 0.1 eq.88
  8.1 0.1 broadcast_add_fusion
  8.2 0.2 bitcast_compare_fusion
  8.4 2.8 %convolution_convert_fusion = bf16[384,2048]{1,0:T(8,128)(2,1)} fusion(pred[384,128]{1,0:T(32,128)(4,1)S(1)} %bitcast_compare_fusion, bf16[128,2048]{1,0:T(8,128)(2,1)} %param.6), kind=kOutput, calls=%fused_computation.15 | convolution fusion | flops 202113024 | bytes 2146304 | tf_op jit(solution)/shard_map/dot_general | solution.py:79
  11.2 4.5 %all-to-all-start = ((bf16[4,96,2048]{2,1,0:T(8,128)(2,1)}), bf16[4,96,2048]{2,1,0:T(8,128)(2,1)}, u32[]{:S(2)}, u32[]{:S(2)}) async-start(bf16[4,96,2048]{2,1,0:T(8,128)(2,1)} %bitcast.66), calls=%async_computation | async-start | bytes 3145728 | tf_op jit(solution)/shard_map/all_to_all | solution.py:70
  15.7 0.1 select_reduce_fusion
  15.8 0.1 mul.86
  15.9 2.8 %multiply_convert_fusion = bf16[384,2048]{1,0:T(8,128)(2,1)} fusion(pred[384,128]{1,0:T(32,128)(4,1)S(1)} %bitcast_compare_fusion, bf16[128,2048]{1,0:T(8,128)(2,1)} %param.11, f32[384]{0:T(512)S(1)} %mul.86), kind=kOutput, calls=%fused_computation.12 | convolution fusion | flops 202899456 | bytes 2147840 | tf_op jit(solution)/shard_map/dot_general | solution.py:82
  18.7 17.7 %all-to-all-done = bf16[4,96,2048]{2,1,0:T(8,128)(2,1)} async-done(((bf16[4,96,2048]{2,1,0:T(8,128)(2,1)}), bf16[4,96,2048]{2,1,0:T(8,128)(2,1)}, u32[]{:S(2)}, u32[]{:S(2)}) %all-to-all-start) | async-done | bytes 1572896 | tf_op jit(solution)/shard_map/all_to_all | solution.py:70
  36.4 4.3 %all-to-all-start.2 = ((bf16[4,96,2048]{2,1,0:T(8,128)(2,1)}), bf16[4,96,2048]{2,1,0:T(8,128)(2,1)}, u32[]{:S(2)}, u32[]{:S(2)}) async-start(bf16[4,96,2048]{2,1,0:T(8,128)(2,1)} %bitcast.65), calls=%async_computation.2 | async-start | bytes 3145728 | tf_op jit(solution)/shard_map/all_to_all | solution.py:70
  40.8 0.0 reduce-scatter.2.cloned.1.call-start
  40.9 2.3 constant_dynamic-slice_fusion.4
  43.2 1.0 pad_maximum_fusion.1
  44.2 2.4 collective-permute-start
  46.5 7.3 %fusion.2 = f32[384,1536]{1,0:T(8,128)} fusion(bf16[384,2048]{1,0:T(8,128)(2,1)} %bitcast.5, bf16[1,2048,1536]{2,1,0:T(8,128)(2,1)} %param.9), kind=kOutput, calls=%fused_computation.2 | convolution fusion | flops 2415919104 | bytes 10223616 | tf_op jit(solution)/shard_map/dot_general | solution.py:103
  53.9 7.1 %all-to-all-done.2 = bf16[4,96,2048]{2,1,0:T(8,128)(2,1)} async-done(((bf16[4,96,2048]{2,1,0:T(8,128)(2,1)}), bf16[4,96,2048]{2,1,0:T(8,128)(2,1)}, u32[]{:S(2)}, u32[]{:S(2)}) %all-to-all-start.2) | async-done | bytes 1572896 | tf_op jit(solution)/shard_map/all_to_all | solution.py:70
  60.9 4.0 %collective-permute-done = bf16[384,1024]{1,0:T(8,128)(2,1)} collective-permute-done((bf16[384,1024]{1,0:T(8,128)(2,1)}, bf16[384,1024]{1,0:T(8,128)(2,1)}, u32[]{:S(2)}, u32[]{:S(2)}) %collective-permute-start) | collective-permute-done | bytes 786464 | tf_op jit(solution)/shard_map/ppermute | solution.py:101
  64.9 3.8 %multiply_convert_fusion.2 = (bf16[384,768]{1,0:T(8,128)(2,1)S(1)}, bf16[384,768]{1,0:T(8,128)(2,1)S(1)}, bf16[384,768]{1,0:T(8,128)(2,1)S(1)}) fusion(f32[384,1536]{1,0:T(8,128)} %fusion.2, bf16[384,2048]{1,0:T(8,128)(2,1)} %bitcast.12, bf16[1,768,2048]{2,1,0:T(8,128)(2,1)S(1)} %copy-done), kind=kOutput, calls=%fused_computation.26 | convolution fusion | flops 1212383232 | bytes 8847360 | tf_op jit(solution)/shard_map/dot_general | solution.py:105
  68.8 3.9 %fusion.37 = f32[768,2048]{1,0:T(8,128)S(1)} fusion(bf16[384,768]{1,0:T(8,128)(2,1)S(1)} %get-tuple-element.17, bf16[384,2048]{1,0:T(8,128)(2,1)} %bitcast.12), kind=kOutput, calls=%fused_computation.72 | convolution fusion | flops 1207959552 | bytes 8454144 | tf_op jit(solution)/shard_map/dot_general | solution.py:107
  72.7 1.4 dynamic-slice_convert_fusion
  74.1 1.7 collective-permute-start.2
  75.9 0.3 collective-permute-start.1
  76.1 1.8 fusion.20
  78.0 12.3 %collective-permute-done.2 = bf16[384,768]{1,0:T(8,128)(2,1)S(1)} collective-permute-done((bf16[384,768]{1,0:T(8,128)(2,1)S(1)}, bf16[384,768]{1,0:T(8,128)(2,1)S(1)}, u32[]{:S(2)}, u32[]{:S(2)}) %collective-permute-start.2) | collective-permute-done | bytes 589856 | tf_op jit(solution)/shard_map/ppermute | solution.py:113
  90.3 11.4 %collective-permute-done.1 = bf16[384,768]{1,0:T(8,128)(2,1)S(1)} collective-permute-done((bf16[384,768]{1,0:T(8,128)(2,1)S(1)}, bf16[384,768]{1,0:T(8,128)(2,1)S(1)}, u32[]{:S(2)}, u32[]{:S(2)}) %collective-permute-start.1) | collective-permute-done | bytes 589856 | tf_op jit(solution)/shard_map/ppermute | solution.py:109
  101.8 4.8 %fusion.4 = bf16[1,1024,1536]{2,1,0:T(8,128)(2,1)} fusion(f32[1024,1536]{1,0:T(8,128)S(1)} %fusion.20, bf16[384,1024]{1,0:T(8,128)(2,1)} %collective-permute-done, bf16[384,768]{1,0:T(8,128)(2,1)S(1)} %collective-permute-done.2, bf16[384,768]{1,0:T(8,128)(2,1)S(1)} %collective-permute-done.1), kind=kOutput, calls=%fused_computation.5 | convolution fusion | flops 1213464576 | bytes 11403264 | tf_op jit(solution)/shard_map/dot_general | solution.py:115
  106.6 1.6 collective-permute-start.3
  108.2 3.6 %fusion.9 = bf16[384,2048]{1,0:T(8,128)(2,1)} fusion(bf16[384,768]{1,0:T(8,128)(2,1)} %copy-done.12, bf16[1,768,2048]{2,1,0:T(8,128)(2,1)S(1)} %copy-done), kind=kOutput, calls=%fused_computation.13 | convolution fusion | flops 1208745984 | bytes 5308416 | tf_op jit(solution)/shard_map/dot_general | solution.py:126
  111.9 4.6 %all-to-all-start.1 = ((bf16[4,96,2048]{2,1,0:T(8,128)(2,1)}), bf16[4,96,2048]{2,1,0:T(8,128)(2,1)}, u32[]{:S(2)}, u32[]{:S(2)}) async-start(bf16[4,96,2048]{2,1,0:T(8,128)(2,1)} %bitcast.68), calls=%async_computation.1 | async-start | bytes 3145728 | tf_op jit(solution)/shard_map/all_to_all | solution.py:70
  116.5 2.4 constant_dynamic-slice_fusion
  118.9 73.8 %collective-permute-done.3 = bf16[4,96,2048]{2,1,0:T(8,128)(2,1)} collective-permute-done((bf16[4,96,2048]{2,1,0:T(8,128)(2,1)}, bf16[4,96,2048]{2,1,0:T(8,128)(2,1)}, u32[]{:S(2)}, u32[]{:S(2)}) %collective-permute-start.3) | collective-permute-done | bytes 1572896 | tf_op jit(solution)/shard_map/ppermute | solution.py:38
  192.8 2.1 bitcast_add_fusion
  194.9 1.6 copy-done.2
  196.5 1.0 fusion.19
  197.6 3.8 %fusion.12 = bf16[384,2048]{1,0:T(8,128)(2,1)} fusion(bf16[1,2048,1536]{2,1,0:T(8,128)(2,1)S(1)} %bitcast.76, bf16[384,768]{1,0:T(8,128)(2,1)S(1)} %copy-done.11, bf16[384,768]{1,0:T(8,128)(2,1)S(1)} %copy-done.9), kind=kOutput, calls=%fused_computation.14 | convolution fusion | flops 2419064832 | bytes 9043968 | tf_op jit(solution)/shard_map/dot_general | solution.py:129
  201.4 4.3 %all-to-all-start.3 = ((bf16[4,96,2048]{2,1,0:T(8,128)(2,1)}), bf16[4,96,2048]{2,1,0:T(8,128)(2,1)}, u32[]{:S(2)}, u32[]{:S(2)}) async-start(bf16[4,96,2048]{2,1,0:T(8,128)(2,1)} %bitcast.67), calls=%async_computation.3 | async-start | bytes 3145728 | tf_op jit(solution)/shard_map/all_to_all | solution.py:70
  205.8 2.1 convert_element_type.74
  207.9 0.7 fusion.31
  208.6 1.2 collective-permute-done.4
  209.8 1.8 bitcast_add_fusion.1
  211.7 1.2 copy-done.3
  212.8 0.8 dynamic-slice_convert_fusion.2
  213.6 3.3 %multiply_reduce_fusion = (f32[2,128]{1,0:T(2,128)}, bf16[128,2048]{1,0:T(8,128)(2,1)}) fusion(f32[128,2048]{1,0:T(8,128)S(1)} %copy-done.5, f32[2,128]{1,0:T(2,128)S(1)} %bitcast.74, bf16[384,2048,1]{1,0,2:T(8,128)(2,1)} %bitcast.10, s32[2,128]{1,0:T(2,128)S(1)} %select_reduce_fusion.2), kind=kOutput, calls=%fused_computation.17 | convolution fusion | flops 404586240 | bytes 3148800 | tf_op jit(solution)/shard_map/dot_general | solution.py:136
  216.9 8.9 %all-to-all-done.3 = bf16[4,96,2048]{2,1,0:T(8,128)(2,1)} async-done(((bf16[4,96,2048]{2,1,0:T(8,128)(2,1)}), bf16[4,96,2048]{2,1,0:T(8,128)(2,1)}, u32[]{:S(2)}, u32[]{:S(2)}) %all-to-all-start.3) | async-done | bytes 1572896 | tf_op jit(solution)/shard_map/all_to_all | solution.py:70
  225.8 2.8 %convolution_convert_fusion.1 = bf16[128,2048]{1,0:T(8,128)(2,1)} fusion(pred[128,384]{1,0:T(8,128)(4,1)} %fusion.31, bf16[384,2048]{1,0:T(8,128)(2,1)} %bitcast.14), kind=kOutput, calls=%fused_computation.16 | convolution fusion | flops 201588736 | bytes 2146304 | tf_op jit(solution)/shard_map/dot_general | solution.py:144
  228.6 4.9 %collective-permute-done.5 = bf16[1,96,2048]{2,1,0:T(8,128)(2,1)S(1)} collective-permute-done((bf16[1,96,2048]{2,1,0:T(8,128)(2,1)}, bf16[1,96,2048]{2,1,0:T(8,128)(2,1)S(1)}, u32[]{:S(2)}, u32[]{:S(2)}) %collective-permute-start.5) | collective-permute-done | bytes 393248 | tf_op jit(solution)/shard_map/ppermute | solution.py:38
  233.5 0.8 add_convert_fusion.1
  (42 shorter events, 0.1 us)
Async XLA Ops:
  7.2 57.7 %copy-start = (bf16[1,768,2048]{2,1,0:T(8,128)(2,1)S(1)}, bf16[1,768,2048]{2,1,0:T(8,128)(2,1)}, u32[]{:S(2)}) copy-start(bf16[1,768,2048]{2,1,0:T(8,128)(2,1)} %param.10) | copy-start | bytes 9437188
  11.2 4.5 %copy-start.13 = (s32[128,2]{0,1:T(2,128)S(1)}, s32[128,2]{0,1:T(2,128)}, u32[]{:S(2)}) copy-start(s32[128,2]{0,1:T(2,128)} %param.7) | copy-start | bytes 3076
  11.2 4.5 %copy-start.14 = (f32[128,2]{0,1:T(2,128)S(1)}, f32[128,2]{0,1:T(2,128)}, u32[]{:S(2)}) copy-start(f32[128,2]{0,1:T(2,128)} %param.8) | copy-start | bytes 3076
  11.2 25.2 %all-to-all-start = ((bf16[4,96,2048]{2,1,0:T(8,128)(2,1)}), bf16[4,96,2048]{2,1,0:T(8,128)(2,1)}, u32[]{:S(2)}, u32[]{:S(2)}) async-start(bf16[4,96,2048]{2,1,0:T(8,128)(2,1)} %bitcast.66), calls=%async_computation | async-start | bytes 3145728 | tf_op jit(solution)/shard_map/all_to_all | solution.py:70
  36.4 24.5 %all-to-all-start.2 = ((bf16[4,96,2048]{2,1,0:T(8,128)(2,1)}), bf16[4,96,2048]{2,1,0:T(8,128)(2,1)}, u32[]{:S(2)}, u32[]{:S(2)}) async-start(bf16[4,96,2048]{2,1,0:T(8,128)(2,1)} %bitcast.65), calls=%async_computation.2 | async-start | bytes 3145728 | tf_op jit(solution)/shard_map/all_to_all | solution.py:70
  40.8 193.6 %reduce-scatter.2.cloned.1.call-start = ((), (), s32[]{:S(2)}) async-start(), calls=%async_computation.5 | async-start | bytes 3932160 | tf_op jit(solution)/shard_map/reduce_scatter | solution.py:118
  44.2 20.7 %collective-permute-start = (bf16[384,1024]{1,0:T(8,128)(2,1)}, bf16[384,1024]{1,0:T(8,128)(2,1)}, u32[]{:S(2)}, u32[]{:S(2)}) collective-permute-start(bf16[384,1024]{1,0:T(8,128)(2,1)} %pad_maximum_fusion.1), channel_id=1, source_target_pairs={{0,4},{4,0},{8,12},{12,8},{16,20},{20,16},{24,28},{28,24},{1,5},{5... | collective-permute-start | bytes 2359304 | tf_op jit(solution)/shard_map/ppermute | solution.py:101
  68.7 3.9 %copy-start.12 = (bf16[384,768]{1,0:T(8,128)(2,1)}, bf16[384,768]{1,0:T(8,128)(2,1)S(1)}, u32[]{:S(2)}) copy-start(bf16[384,768]{1,0:T(8,128)(2,1)S(1)} %get-tuple-element.17) | copy-start | bytes 1769476
  68.7 7.4 %copy-start.8 = (bf16[384,768]{1,0:T(8,128)(2,1)}, bf16[384,768]{1,0:T(8,128)(2,1)S(1)}, u32[]{:S(2)}) copy-start(bf16[384,768]{1,0:T(8,128)(2,1)S(1)} %get-tuple-element.15) | copy-start | bytes 1769476
  68.7 7.4 %copy-start.10 = (bf16[384,768]{1,0:T(8,128)(2,1)}, bf16[384,768]{1,0:T(8,128)(2,1)S(1)}, u32[]{:S(2)}) copy-start(bf16[384,768]{1,0:T(8,128)(2,1)S(1)} %get-tuple-element.11) | copy-start | bytes 1769476
  72.7 5.3 %copy-start.1 = (f32[768,2048]{1,0:T(8,128)}, f32[768,2048]{1,0:T(8,128)S(1)}, u32[]{:S(2)}) copy-start(f32[768,2048]{1,0:T(8,128)S(1)} %fusion.37) | copy-start | bytes 18874372
  72.7 3.5 %copy-start.6 = (bf16[384,256]{1,0:T(8,128)(2,1)S(1)}, bf16[384,256]{1,0:T(8,128)(2,1)}, u32[]{:S(2)}) copy-start(bf16[384,256]{1,0:T(8,128)(2,1)} %get-tuple-element.20) | copy-start | bytes 589828
  72.7 3.5 %copy-start.7 = (bf16[384,256]{1,0:T(8,128)(2,1)S(1)}, bf16[384,256]{1,0:T(8,128)(2,1)}, u32[]{:S(2)}) copy-start(bf16[384,256]{1,0:T(8,128)(2,1)} %get-tuple-element.21) | copy-start | bytes 589828
  74.1 16.2 %collective-permute-start.2 = (bf16[384,768]{1,0:T(8,128)(2,1)S(1)}, bf16[384,768]{1,0:T(8,128)(2,1)S(1)}, u32[]{:S(2)}, u32[]{:S(2)}) collective-permute-start(bf16[384,768]{1,0:T(8,128)(2,1)S(1)} %get-tuple-element.11), channel_id=1, source_target_pairs={{0,4},{4,0},{8,12},{12,8},{16,20},{20,16},{24,28},{28,24},{1,5},{5... | collective-permute-start | bytes 1769480 | tf_op jit(solution)/shard_map/ppermute | solution.py:113
  75.9 25.9 %collective-permute-start.1 = (bf16[384,768]{1,0:T(8,128)(2,1)S(1)}, bf16[384,768]{1,0:T(8,128)(2,1)S(1)}, u32[]{:S(2)}, u32[]{:S(2)}) collective-permute-start(bf16[384,768]{1,0:T(8,128)(2,1)S(1)} %get-tuple-element.15), channel_id=1, source_target_pairs={{0,4},{4,0},{8,12},{12,8},{16,20},{20,16},{24,28},{28,24},{1,5},{5... | collective-permute-start | bytes 1769480 | tf_op jit(solution)/shard_map/ppermute | solution.py:109
  106.6 86.1 %collective-permute-start.3 = (bf16[4,96,2048]{2,1,0:T(8,128)(2,1)}, bf16[4,96,2048]{2,1,0:T(8,128)(2,1)}, u32[]{:S(2)}, u32[]{:S(2)}) collective-permute-start(bf16[4,96,2048]{2,1,0:T(8,128)(2,1)} %bitcast.69), channel_id=1, source_target_pairs={{0,8},{4,12},{8,0},{12,4},{16,24},{20,28},{24,16},{28,20},{1,9},{5... | collective-permute-start | bytes 4718600 | tf_op jit(solution)/shard_map/ppermute | solution.py:38
  111.9 89.5 %all-to-all-start.1 = ((bf16[4,96,2048]{2,1,0:T(8,128)(2,1)}), bf16[4,96,2048]{2,1,0:T(8,128)(2,1)}, u32[]{:S(2)}, u32[]{:S(2)}) async-start(bf16[4,96,2048]{2,1,0:T(8,128)(2,1)} %bitcast.68), calls=%async_computation.1 | async-start | bytes 3145728 | tf_op jit(solution)/shard_map/all_to_all | solution.py:70
  116.5 81.0 %slice-start = ((s8[6291456]{0:T(1024)(128)(4,1)}), s8[4194304]{0:T(1024)(128)(4,1)S(1)}, s32[]{:S(2)}) async-start(s8[6291456]{0:T(1024)(128)(4,1)} %bitcast.75), calls=%async_computation.6 | async-start | bytes 8388608
  118.9 78.6 %slice-start.1 = ((s8[6291456]{0:T(1024)(128)(4,1)}), s8[2097152]{0:T(1024)(128)(4,1)S(1)}, s32[]{:S(2)}) async-start(s8[6291456]{0:T(1024)(128)(4,1)} %bitcast.75), calls=%async_computation.7 | async-start | bytes 4194304
  194.9 1.7 copy-start.2
  194.9 2.6 %copy-start.9 = (bf16[384,768]{1,0:T(8,128)(2,1)S(1)}, bf16[384,768]{1,0:T(8,128)(2,1)}, u32[]{:S(2)}) copy-start(bf16[384,768]{1,0:T(8,128)(2,1)} %copy-done.8) | copy-start | bytes 1769476
  194.9 2.6 %copy-start.11 = (bf16[384,768]{1,0:T(8,128)(2,1)S(1)}, bf16[384,768]{1,0:T(8,128)(2,1)}, u32[]{:S(2)}) copy-start(bf16[384,768]{1,0:T(8,128)(2,1)} %copy-done.10) | copy-start | bytes 1769476
  197.5 12.3 %collective-permute-start.4 = (bf16[2,96,2048]{2,1,0:T(8,128)(2,1)}, bf16[2,96,2048]{2,1,0:T(8,128)(2,1)}, u32[]{:S(2)}, u32[]{:S(2)}) collective-permute-start(bf16[2,96,2048]{2,1,0:T(8,128)(2,1)} %fusion.19), channel_id=1, source_target_pairs={{0,4},{4,0},{8,12},{12,8},{16,20},{20,16},{24,28},{28,24},{1,5},{5... | collective-permute-start | bytes 2359304 | tf_op jit(solution)/shard_map/ppermute | solution.py:38
  201.4 24.5 %all-to-all-start.3 = ((bf16[4,96,2048]{2,1,0:T(8,128)(2,1)}), bf16[4,96,2048]{2,1,0:T(8,128)(2,1)}, u32[]{:S(2)}, u32[]{:S(2)}) async-start(bf16[4,96,2048]{2,1,0:T(8,128)(2,1)} %bitcast.67), calls=%async_computation.3 | async-start | bytes 3145728 | tf_op jit(solution)/shard_map/all_to_all | solution.py:70
  208.6 5.0 %copy-start.5 = (f32[128,2048]{1,0:T(8,128)S(1)}, f32[128,2048]{1,0:T(8,128)}, u32[]{:S(2)}) copy-start(f32[128,2048]{1,0:T(8,128)} %convert_element_type.74) | copy-start | bytes 3145732
  211.7 1.2 copy-start.3
  213.6 19.9 %collective-permute-start.5 = (bf16[1,96,2048]{2,1,0:T(8,128)(2,1)}, bf16[1,96,2048]{2,1,0:T(8,128)(2,1)S(1)}, u32[]{:S(2)}, u32[]{:S(2)}) collective-permute-start(bf16[1,96,2048]{2,1,0:T(8,128)(2,1)} %dynamic-slice_convert_fusion.2), channel_id=1, source_target_pairs={{0,16},{4,20},{8,24},{12,28},{16,0},{20,4},{24,8},{28,12},{1,17},{... | collective-permute-start | bytes 1179656 | tf_op jit(solution)/shard_map/ppermute | solution.py:38
  225.8 7.7 %copy-start.4 = (f32[2,96,2048]{2,1,0:T(8,128)S(1)}, f32[2,96,2048]{2,1,0:T(8,128)}, u32[]{:S(2)}) copy-start(f32[2,96,2048]{2,1,0:T(8,128)} %copy-done.3) | copy-start | bytes 4718596
Sparse Core Ops, SparseCore 0:
  106.7 86.8 reduce-scatter.1
